TPU v7x, 256 devices: a whole 4x4x8 slice. The times are simulated.
256 devices in a mesh: pipe: 4 (over z_hi), expert: 64 (over y, z_lo, x, core).
Axes of the slice: x: 4, y: 4, z: 8 (z_hi: 4, z_lo: 2; z = z_hi * 2 + z_lo), core: 2. Of those that a mesh axis runs over, the one named last changes fastest.
Arguments:
- forward_rows: bfloat16 [4, 4096, 3584], P('pipe', 'expert'), may hold values from -6 to 6
- forward_routes: int32 [4, 4096, 2], P('pipe', 'expert'), may hold values from 0 to 31, all different within a row; in each aligned block of 64 rows (0 to 63, 64 to 127, ..., all dimensions but the last counted through in order) at most 5 rows name the same one
- saved_rows: bfloat16 [4, 4096, 3584], P('pipe', 'expert'), may hold values from -6 to 6
- cotangent: bfloat16 [4, 4096, 3584], P('pipe', 'expert'), may hold values from -6 to 6
- backward_routes: int32 [4, 4096, 2], P('pipe', 'expert'), may hold values from 0 to 31, all different within a row; in each aligned block of 64 rows (0 to 63, 64 to 127, ..., all dimensions but the last counted through in order) at most 5 rows name the same one
- norm_gain: float32 [4, 3584], P('pipe'), may hold values from 0.1 to 1.9
- router: bfloat16 [4, 3584, 32], P('pipe'), may hold values from -0.09375 to 0.09375
- gate_weight: bfloat16 [4, 64, 3584, 512], P('pipe', 'expert'), may hold values from -0.09375 to 0.09375
- up_weight: bfloat16 [4, 64, 3584, 512], P('pipe', 'expert'), may hold values from -0.09375 to 0.09375
- down_weight: bfloat16 [4, 64, 512, 3584], P('pipe', 'expert'), may hold values from -0.1875 to 0.1875
Outputs:
- forward_next: bfloat16 [4, 4096, 3584], P('pipe', 'expert')
- backward_next: bfloat16 [4, 4096, 3584], P('pipe', 'expert')
Inputs may be any that keep to these rules, and one draw needn't show every extreme that they name: `forward_routes`: each row names 2 different experts. Within the rows of one device (aligned blocks of 64 rows) no expert is named more than 5 times, a bound that some block reaches. `backward_routes`: as forward_routes.
All inputs are finite; a program needn't handle non-finite values.
Results may differ from a plain program's by a relative error of at most 0.007.
Values may be sent and summed in bfloat16 or wider, within the bound.
No kernel may reach another device: no remote copies, remote signals or barrier semaphores. Data moves between devices by JAX's collectives and lax.ppermute only.
A program may use at most 128 MiB of HBM per device.

v0:
```python
import jax
import jax.numpy as jnp
import numpy as np
from jax import lax
from jax.experimental import pallas as pl
from jax.experimental.pallas import tpu as pltpu
from jax.sharding import PartitionSpec as P

epsilon = 1e-06
VMEM_LIMIT = 32 * 1024 * 1024
CAP = 5
LANES = 1152
ROWS = 16
TAIL = 3 * LANES
FAR = pl.BlockSpec(memory_space=pltpu.HBM)
NEAR = pl.BlockSpec(memory_space=pltpu.VMEM)


def selections():
    body = np.zeros((3, 16, CAP, 16, ROWS), np.float32)
    tail = np.zeros((CAP, 16, CAP, 16, ROWS), np.float32)
    for i in range(16):
        for s in range(CAP):
            tail[s, i, s, i, 15] = 1
            for g in range(3):
                body[g, i, s, i, 5 * g + s] = 1
    body, tail = body.reshape(240, 256), tail.reshape(400, 256)
    gather = np.concatenate([body, tail])
    scatter = np.concatenate([body.T] + [tail[80 * s : 80 * s + 80].T for s in range(CAP)], axis=1)
    scatter = np.concatenate([scatter, tail.reshape(CAP, 80, 256).sum(0).T], axis=1)
    blocks = [scatter[:, :240]] + [scatter[:, 240 + 80 * n : 320 + 80 * n] for n in range(CAP + 1)]
    scatter = np.concatenate([np.pad(b, ((0, 0), (0, 240 - b.shape[1]))) for b in blocks])
    return jnp.asarray(gather, jnp.bfloat16), jnp.asarray(scatter, jnp.bfloat16)


def params():
    return dict(
        compiler_params=pltpu.CompilerParams(vmem_limit_bytes=VMEM_LIMIT),
        cost_estimate=pl.CostEstimate(flops=0, bytes_accessed=1024, transcendentals=0),
    )


def f32(x):
    return x.astype(jnp.float32)


def count(hits, axis):
    return jnp.sum(jnp.where(hits, 1.0, 0.0), axis=axis, keepdims=True)


def place_of(position):
    expert = lax.bitwise_and(lax.shift_right_logical(position, 4), 31)
    row = lax.bitwise_and(position, 15)
    block = jnp.where(row >= 5, 1, 0) + jnp.where(row >= 10, 1, 0) + jnp.where(row >= 15, 1, 0)
    return expert, row, block, row - 5 * block


def pack(units, gain, ids, after=()):
    n, m = len(units), len(after)
    tokens, width = units[0][0].shape
    half_rows = 32 * ROWS
    ids = ids.astype(jnp.float32)
    ids_rows = jnp.concatenate([ids, ids]).T

    def kernel(*refs):
        rows, (gain_ref, ids_c, ids_r) = refs[:n], refs[n : n + 3]
        out, made, low, high, sems = refs[n + 3 + m :]
        first, second = ids_c[:, 0:1], ids_c[:, 1:2]
        first_r, second_r = ids_r[0:1, :], ids_r[1:2, :]
        shape = (tokens, 2 * tokens)
        token = lax.broadcasted_iota(jnp.int32, shape, 0)
        before = token < lax.bitwise_and(lax.broadcasted_iota(jnp.int32, shape, 1), tokens - 1)
        slot_0 = count((first == first_r) & before, 0)
        slot_1 = count(first == second_r, 0) + count((second == second_r) & before, 0)
        key_0, key_1 = first_r * 8 + slot_0, second_r * 8 + slot_1
        shape = (half_rows, 2 * tokens)
        expert, row, block, slot = place_of(lax.broadcasted_iota(jnp.int32, shape, 0))
        right = lax.broadcasted_iota(jnp.int32, shape, 1) >= tokens

        def hits(key):
            key = f32(key)
            return (key_0 == key) | (key_1 == key)

        def matrix(mask):
            return jnp.where(mask, 1.0, 0.0).astype(jnp.bfloat16)

        own = hits(expert * 8 + slot)
        pick_low = matrix(own & (block == jnp.where(right, 1, 0)))
        third = own & (block == 2) & ~right
        pick_rest = matrix(third)
        picks = [
            matrix(third | (hits(expert * 8 + s) & (row == 15) & right)) for s in range(CAP)
        ]
        for u in range(n):
            x = rows[u][...]
            if units[u][1]:
                v = f32(x)
                inverse = lax.rsqrt(jnp.mean(v * v, axis=-1, keepdims=True) + epsilon)
                x = (v * inverse * gain_ref[...]).astype(jnp.bfloat16)
            low[0:tokens, :] = x[:, :LANES]
            low[tokens:, :] = x[:, LANES : 2 * LANES]
            high[0:tokens, :] = x[:, 2 * LANES : TAIL]
            high[tokens:, :] = jnp.zeros((tokens, LANES), jnp.bfloat16)
            for s in range(CAP):
                high[tokens:, 128 * s : 128 * s + 128] = x[:, TAIL:]
            for s in range(9):
                cols = slice(128 * s, 128 * s + 128)
                part = jnp.dot(pick_low, low[:, cols], preferred_element_type=jnp.float32)
                part += jnp.dot(
                    picks[s] if s < CAP else pick_rest,
                    high[:, cols],
                    preferred_element_type=jnp.float32,
                )
                made[:, u * LANES + 128 * s : u * LANES + 128 * s + 128] = part.astype(
                    jnp.bfloat16
                )
        stores = [
            pltpu.make_async_copy(made, out.at[pl.ds(half_rows * r, half_rows)], sems.at[r])
            for r in range(2)
        ]
        for store in stores:
            store.start()
        for store in stores:
            store.wait()

    return pl.pallas_call(
        kernel,
        out_shape=jax.ShapeDtypeStruct((2 * half_rows, n * LANES), jnp.bfloat16),
        in_specs=[NEAR] * (n + 3) + [pl.BlockSpec(memory_space=pl.ANY)] * m,
        out_specs=FAR,
        scratch_shapes=[
            pltpu.VMEM((half_rows, n * LANES), jnp.bfloat16),
            pltpu.VMEM((2 * tokens, LANES), jnp.bfloat16),
            pltpu.VMEM((2 * tokens, LANES), jnp.bfloat16),
            pltpu.SemaphoreType.DMA((2,)),
        ],
        **params(),
    )(*[rows for rows, _ in units], gain, ids, ids_rows, *after)


def unpack(chunks, gather, x, offset, start):
    def step(b, carry):
        held = pl.ds(pl.multiple_of(256 * b, 256), 256)
        rows = pl.ds(pl.multiple_of(80 * b, 16), 80)
        for c in range(3):
            part = jnp.dot(
                gather[:240, :],
                chunks[held, offset + 384 * c : offset + 384 * c + 384],
                preferred_element_type=jnp.float32,
            ).astype(jnp.bfloat16)
            for g in range(3):
                at = start + g * LANES + 384 * c
                x[rows, at : at + 384] = part[80 * g : 80 * g + 80]
        total = jnp.zeros((80, 128), jnp.float32)
        for s in range(CAP):
            total += jnp.dot(
                gather[240 + 80 * s : 320 + 80 * s, :],
                chunks[held, offset + 128 * s : offset + 128 * s + 128],
                preferred_element_type=jnp.float32,
            )
        x[rows, start + TAIL : start + TAIL + 128] = total.astype(jnp.bfloat16)
        return carry

    lax.fori_loop(0, 4, step, 0)


def repack(chunks, scatter, made, rest, extra=None):
    def step(b, carry):
        held = pl.ds(pl.multiple_of(256 * b, 256), 256)
        stacked = pl.ds(pl.multiple_of(240 * b, 16), 240)
        rows = pl.ds(pl.multiple_of(80 * b, 16), 80)
        for s in range(9):
            cols = slice(128 * s, 128 * s + 128)
            part = jnp.dot(scatter[:256, :], made[stacked, cols], preferred_element_type=jnp.float32)
            source = rest if s < CAP else extra if s == CAP else None
            if source is not None:
                part += jnp.dot(
                    scatter[256 + 256 * s : 512 + 256 * s, :80],
                    source[rows, :],
                    preferred_element_type=jnp.float32,
                )
            chunks[held, cols] = part.astype(jnp.bfloat16)
        return carry

    lax.fori_loop(0, 4, step, 0)


def put_result(made, rest, product):
    def step(c, carry):
        for g in range(3):
            cols = pl.ds(pl.multiple_of(g * LANES + 384 * c, 128), 384)
            part = product(cols).astype(jnp.bfloat16)
            at = pl.ds(pl.multiple_of(384 * c, 128), 384)
            for b in range(4):
                made[240 * b + 80 * g : 240 * b + 80 * g + 80, at] = part[80 * b : 80 * b + 80]
        return carry

    lax.fori_loop(0, 3, step, 0)
    rest[...] = product(pl.ds(TAIL, 128)).astype(jnp.bfloat16)


def expert_forward(chunks, tables, w_gate, w_up, w_down, after=()):
    width, units = w_gate.shape
    m = len(after)

    def kernel(far, gather, scatter, wg, wu, wd, *refs):
        far_out, near, x, hidden, made, rest, sems = refs[m:]
        load = pltpu.make_async_copy(far, near, sems.at[0])
        load.start()
        load.wait()
        unpack(near, gather, x, 0, 0)

        def first(k, carry):
            cols = pl.ds(pl.multiple_of(k * 256, 256), 256)
            gate = jnp.dot(x[...], wg[:, cols], preferred_element_type=jnp.float32)
            upper = jnp.dot(x[...], wu[:, cols], preferred_element_type=jnp.float32)
            hidden[:, cols] = (gate * jax.nn.sigmoid(gate) * upper).astype(jnp.bfloat16)
            return carry

        lax.fori_loop(0, units // 256, first, 0)
        put_result(
            made,
            rest,
            lambda cols: jnp.dot(hidden[...], wd[:, cols], preferred_element_type=jnp.float32),
        )
        repack(near, scatter, made, rest)
        store = pltpu.make_async_copy(near, far_out, sems.at[1])
        store.start()
        store.wait()

    return pl.pallas_call(
        kernel,
        out_shape=jax.ShapeDtypeStruct(chunks.shape, jnp.bfloat16),
        in_specs=[FAR] + [NEAR] * 5 + [pl.BlockSpec(memory_space=pl.ANY)] * m,
        out_specs=FAR,
        scratch_shapes=[
            pltpu.VMEM(chunks.shape, jnp.bfloat16),
            pltpu.VMEM((320, width), jnp.bfloat16),
            pltpu.VMEM((320, units), jnp.bfloat16),
            pltpu.VMEM((960, LANES), jnp.bfloat16),
            pltpu.VMEM((320, 128), jnp.bfloat16),
            pltpu.SemaphoreType.DMA((2,)),
        ],
        **params(),
    )(chunks, *tables, w_gate, w_up, w_down, *after)


def expert_backward(chunks, tables, w_gate, w_up, w_down):
    width, units = w_gate.shape
    contract = (((1,), (1,)), ((), ()))

    def kernel(far, gather, scatter, wg, wu, wd, far_out, near, x, d_gate, d_up, made, rest, extra, sems):
        load = pltpu.make_async_copy(far, near, sems.at[0])
        load.start()
        load.wait()
        unpack(near, gather, x, 0, 0)
        unpack(near, gather, x, LANES, width)

        def first(k, inner):
            cols = pl.ds(pl.multiple_of(k * 256, 256), 256)
            gate = jnp.dot(x[:, :width], wg[:, cols], preferred_element_type=jnp.float32)
            upper = jnp.dot(x[:, :width], wu[:, cols], preferred_element_type=jnp.float32)
            s = jax.nn.sigmoid(gate)
            d_hidden = lax.dot_general(
                x[:, width:], wd[cols, :], contract, preferred_element_type=jnp.float32
            )
            active = gate * s
            hidden = f32((active * upper).astype(jnp.bfloat16))
            d_gate[:, cols] = (d_hidden * upper * s * (1.0 + gate * (1.0 - s))).astype(
                jnp.bfloat16
            )
            d_up[:, cols] = (d_hidden * active).astype(jnp.bfloat16)
            return inner + jnp.sum(hidden * d_hidden, axis=1, keepdims=True)

        inner = lax.fori_loop(0, units // 256, first, jnp.zeros((320, 1), jnp.float32))
        slot = lax.rem(lax.broadcasted_iota(jnp.int32, (320, 128), 0), CAP)
        lane = lax.broadcasted_iota(jnp.int32, (320, 128), 1)
        extra[...] = jnp.where(slot == lane, inner, 0.0).astype(jnp.bfloat16)

        def product(cols):
            return lax.dot_general(
                d_gate[...], wg[cols, :], contract, preferred_element_type=jnp.float32
            ) + lax.dot_general(
                d_up[...], wu[cols, :], contract, preferred_element_type=jnp.float32
            )

        put_result(made, rest, product)
        repack(near, scatter, made, rest, extra)
        store = pltpu.make_async_copy(near.at[:, pl.ds(0, LANES)], far_out, sems.at[1])
        store.start()
        store.wait()

    return pl.pallas_call(
        kernel,
        out_shape=jax.ShapeDtypeStruct((chunks.shape[0], LANES), jnp.bfloat16),
        in_specs=[FAR] + [NEAR] * 5,
        out_specs=FAR,
        scratch_shapes=[
            pltpu.VMEM(chunks.shape, jnp.bfloat16),
            pltpu.VMEM((320, 2 * width), jnp.bfloat16),
            pltpu.VMEM((320, units), jnp.bfloat16),
            pltpu.VMEM((320, units), jnp.bfloat16),
            pltpu.VMEM((960, LANES), jnp.bfloat16),
            pltpu.VMEM((320, 128), jnp.bfloat16),
            pltpu.VMEM((320, 128), jnp.bfloat16),
            pltpu.SemaphoreType.DMA((2,)),
        ],
        **params(),
    )(chunks, *tables, w_gate, w_up, w_down)


def combine(chunks, weights, ids, base=None):
    tokens = ids.shape[0]
    width = TAIL + 128
    total_rows = chunks.shape[0]
    ids = ids.astype(jnp.float32)
    forward = base is not None

    def kernel(far, w, ids_c, ids_r, *refs):
        if forward:
            base_ref, out, near, parts, tails, sem = refs
        else:
            out, inner_out, near, parts, tails, sem = refs
        load = pltpu.make_async_copy(far, near, sem)
        load.start()
        first, second = ids_c[:, 0:1], ids_c[:, 1:2]
        first_r, second_r = ids_r[0:1, :], ids_r[1:2, :]
        shape = (tokens, tokens)
        before = lax.broadcasted_iota(jnp.int32, shape, 1) < lax.broadcasted_iota(
            jnp.int32, shape, 0
        )
        slot_0 = count((first == first_r) & before, 1)
        slot_1 = count(second == first_r, 1) + count((second == second_r) & before, 1)
        key_0, key_1 = first * 8 + slot_0, second * 8 + slot_1
        shape = (tokens, total_rows)
        expert, row, block, slot = place_of(lax.broadcasted_iota(jnp.int32, shape, 1))

        def spread(key):
            key = f32(key)
            total = jnp.where(key_0 == key, w[:, 0:1], 0.0) + jnp.where(
                key_1 == key, w[:, 1:2], 0.0
            )
            upper = f32(total.astype(jnp.bfloat16))
            return upper, total - upper

        def put(ref, at, values, mask):
            for n, value in enumerate(values):
                ref[at + tokens * n : at + tokens * n + tokens, :] = jnp.where(
                    mask, value, 0.0
                ).astype(jnp.bfloat16)

        values = spread(expert * 8 + slot)
        for g in range(3):
            put(parts, 2 * tokens * g, values, block == g)
        for s in range(CAP):
            put(tails, 2 * tokens * s, spread(expert * 8 + s), row == 15)
        load.wait()
        if not forward:
            lane = f32(lax.broadcasted_iota(jnp.int32, (tokens, 128), 1))
            for k, (chosen, at) in enumerate(((first, slot_0), (second, slot_1))):
                pick = jnp.where((row == 15) & (f32(expert) == chosen), 1.0, 0.0)
                found = jnp.dot(
                    pick.astype(jnp.bfloat16), near[:, 640:768], preferred_element_type=jnp.float32
                )
                inner_out[:, 128 * k : 128 * k + 128] = jnp.broadcast_to(
                    jnp.sum(jnp.where(lane == at, found, 0.0), axis=1, keepdims=True),
                    (tokens, 128),
                )

        def store(at, size, value):
            if forward:
                value = f32(base_ref[:, at : at + size]) + value
            out[:, at : at + size] = value.astype(out.dtype)

        for c in range(3):
            part = jnp.dot(
                parts[...], near[:, 384 * c : 384 * c + 384], preferred_element_type=jnp.float32
            )
            for g in range(3):
                at = 2 * tokens * g
                store(
                    g * LANES + 384 * c,
                    384,
                    part[at : at + tokens] + part[at + tokens : at + 2 * tokens],
                )
        total = jnp.zeros((2 * tokens, 128), jnp.float32)
        for s in range(CAP):
            total += jnp.dot(
                tails[2 * tokens * s : 2 * tokens * (s + 1), :],
                near[:, 128 * s : 128 * s + 128],
                preferred_element_type=jnp.float32,
            )
        store(TAIL, 128, total[:tokens] + total[tokens:])

    outs = [jax.ShapeDtypeStruct((tokens, width), jnp.bfloat16 if forward else jnp.float32)]
    if not forward:
        outs.append(jax.ShapeDtypeStruct((tokens, 256), jnp.float32))
    operands = [weights, ids, ids.T] + ([base] if forward else [])
    return pl.pallas_call(
        kernel,
        out_shape=outs,
        in_specs=[FAR] + [NEAR] * len(operands),
        out_specs=[NEAR] * len(outs),
        scratch_shapes=[
            pltpu.VMEM(chunks.shape, jnp.bfloat16),
            pltpu.VMEM((6 * tokens, total_rows), jnp.bfloat16),
            pltpu.VMEM((2 * CAP * tokens, total_rows), jnp.bfloat16),
            pltpu.SemaphoreType.DMA,
        ],
        **params(),
    )(chunks, *operands)


def swapped(chunks):
    shape = chunks.shape
    chunks = chunks.reshape(shape[0] // ROWS, ROWS, shape[1])
    return lax.all_to_all(chunks, "expert", 0, 0, tiled=True).reshape(shape)


def passed_along(x, axis, by):
    n = lax.axis_size(axis)
    return lax.ppermute(x, axis, [(i, (i + by) % n) for i in range(n)])


def normalise(values, gain_row):
    inverse = lax.rsqrt(jnp.mean(values * values, axis=-1, keepdims=True) + epsilon)
    return values * inverse * gain_row


def gates(normed, router_map, routes):
    logits = jnp.dot(normed, router_map.astype(jnp.float32), precision=lax.Precision.HIGHEST)
    scores = jax.nn.sigmoid(logits)
    choices_axis = jnp.arange(router_map.shape[1], dtype=jnp.int32)
    onehot = (routes[:, :, None] == choices_axis[None, None, :]).astype(scores.dtype)
    picked = jnp.sum(onehot * scores[:, None, :], axis=-1)
    return picked / jnp.sum(picked, axis=1, keepdims=True)


def body(
    forward_rows,
    forward_routes,
    saved_rows,
    cotangent,
    backward_routes,
    norm_gain,
    router,
    gate_weight,
    up_weight,
    down_weight,
):
    gain_row, router_map = norm_gain[0], router[0]
    weights = (gate_weight[0, 0], up_weight[0, 0], down_weight[0, 0])
    tables = selections()
    backward_ids, forward_ids = backward_routes[0], forward_routes[0]

    both_out = pack([(saved_rows[0], True), (cotangent[0], False)], norm_gain, backward_ids)
    forward_out = pack([(forward_rows[0], True)], norm_gain, forward_ids, after=[both_out])
    both_in = swapped(both_out)
    forward_in = swapped(forward_out)
    backward_chunks = expert_backward(both_in, tables, *weights)
    backward_back = swapped(backward_chunks)
    forward_chunks = expert_forward(forward_in, tables, *weights, after=[backward_chunks])
    forward_back = swapped(forward_chunks)

    normed, norm_back = jax.vjp(
        lambda v: normalise(v, gain_row), saved_rows[0].astype(jnp.float32)
    )
    backward_weights, gate_back = jax.vjp(lambda v: gates(v, router_map, backward_ids), normed)
    forward_weights = gates(
        normalise(forward_rows[0].astype(jnp.float32), gain_row), router_map, forward_ids
    )
    d_normed, inner = combine(backward_back, backward_weights, backward_ids)
    (d_from_gates,) = gate_back(jnp.stack([inner[:, 0], inner[:, 128]], axis=1))
    (d_rows,) = norm_back(d_normed + d_from_gates)
    gradient = (cotangent[0].astype(jnp.float32) + d_rows).astype(jnp.bfloat16)
    backward_next = passed_along(gradient[None], "pipe", -1)
    (result,) = combine(forward_back, forward_weights, forward_ids, forward_rows[0])
    forward_next = passed_along(result[None], "pipe", 1)
    return (forward_next, backward_next)


def solution(mesh):
    in_specs = (
        P("pipe", "expert", None),
        P("pipe", "expert", None),
        P("pipe", "expert", None),
        P("pipe", "expert", None),
        P("pipe", "expert", None),
        P("pipe", None),
        P("pipe", None, None),
        P("pipe", "expert", None, None),
        P("pipe", "expert", None, None),
        P("pipe", "expert", None, None),
    )
    out_specs = (P("pipe", "expert", None), P("pipe", "expert", None))
    return jax.shard_map(body, mesh=mesh, in_specs=in_specs, out_specs=out_specs, check_vma=False)
```

profile of v0, /device:TPU:41, one launch (start us, length us, event | category | flops | bytes accessed | tf_op | source)
XLA Modules:
  0.0 246.0 jit_solution(12101819394690223012)
XLA Ops:
  0.6 1.3 fusion.31
  2.1 1.0 copy-done.11
  3.1 1.0 copy-done.16
  4.2 0.7 copy-done.23
  4.9 2.3 shard_map.131.refs_4_
  7.2 2.2 copy-done.1
  9.4 9.5 %all-to-all-start.1 = ((bf16[64,16,2304]{2,1,0:T(8,128)(2,1)}), bf16[64,16,2304]{2,1,0:T(8,128)(2,1)}, u32[]{:S(2)}, u32[]{:S(2)}) async-start(bf16[64,16,2304]{2,1,0:T(8,128)(2,1)} %bitcast.53), calls=%async_computation.1 | async-start | bytes 9437184 | tf_op jit(solution)/shard_map/all_to_all | solution.py:417
  19.7 2.3 copy-done.2
  22.0 1.8 shard_map.132
  23.9 1.4 copy-done.9
  25.3 51.9 %all-to-all-done.1 = bf16[64,16,2304]{2,1,0:T(8,128)(2,1)} async-done(((bf16[64,16,2304]{2,1,0:T(8,128)(2,1)}), bf16[64,16,2304]{2,1,0:T(8,128)(2,1)}, u32[]{:S(2)}, u32[]{:S(2)}) %all-to-all-start.1) | async-done | bytes 4718624 | tf_op jit(solution)/shard_map/all_to_all | solution.py:417
  77.2 7.0 %all-to-all-start = ((bf16[64,16,1152]{2,1,0:T(8,128)(2,1)}), bf16[64,16,1152]{2,1,0:T(8,128)(2,1)S(1)}, u32[]{:S(2)}, u32[]{:S(2)}) async-start(bf16[64,16,1152]{2,1,0:T(8,128)(2,1)} %bitcast.62), calls=%async_computation | async-start | bytes 4718592 | tf_op jit(solution)/shard_map/all_to_all | solution.py:417
  84.3 2.0 copy-done.3
  86.3 2.0 copy-done.5
  88.3 2.0 copy-done.7
  90.4 1.2 copy-done.14
  91.6 17.4 %shard_map.133.refs_0_ = bf16[1024,1152]{1,0:T(8,128)(2,1)} custom-call(bf16[1024,2304]{1,0:T(8,128)(2,1)} %bitcast.13.far, bf16[640,256]{1,0:T(8,128)(2,1)S(1)} %copy-done.18, bf16[1792,240]{1,0:T(8,128)(2,1)S(1)} %copy-done.14, bf16[3584,512]{1,0:T(8,128)(2,1)S(1)} %bitcast.54, bf16[3584,512]{1,0:T(8,128)(2,1)S(1)} %bitcast.56, bf16[512,3584]{1,0:T(8,128)(2,1)S(1)} %bitcast.58), custom_call_target="tpu_custom_call" | custom-call | bytes 1024 | tf_op jit(solution)/shard_map/pallas_call | solution.py:293
  109.0 6.1 %all-to-all-done = bf16[64,16,1152]{2,1,0:T(8,128)(2,1)S(1)} async-done(((bf16[64,16,1152]{2,1,0:T(8,128)(2,1)}), bf16[64,16,1152]{2,1,0:T(8,128)(2,1)S(1)}, u32[]{:S(2)}, u32[]{:S(2)}) %all-to-all-start) | async-done | bytes 2359328 | tf_op jit(solution)/shard_map/all_to_all | solution.py:417
  115.1 2.0 copy-done.4
  117.2 2.0 copy-done.6
  119.2 2.0 copy-done.8
  121.2 1.2 copy-done.15
  122.4 9.2 %shard_map.134 = bf16[1024,1152]{1,0:T(8,128)(2,1)S(1)} custom-call(bf16[1024,1152]{1,0:T(8,128)(2,1)S(1)} %bitcast.60, bf16[640,256]{1,0:T(8,128)(2,1)S(1)} %copy-done.18, bf16[1792,240]{1,0:T(8,128)(2,1)S(1)} %copy-done.15, bf16[3584,512]{1,0:T(8,128)(2,1)S(1)} %bitcast.55, bf16[3584,512]{1,0:T(8,128)(2,1)S(1)} %bitcast.57, ...), custom_call_target="tpu_custom_call" | custom-call | bytes 1024 | tf_op jit(solution)/shard_map/pallas_call | solution.py:231
  131.6 36.3 %all_to_all.20 = bf16[64,16,1152]{2,1,0:T(8,128)(2,1)} all-to-all(bf16[64,16,1152]{2,1,0:T(8,128)(2,1)S(1)} %bitcast.61), channel_id=1, replica_groups=mesh['pipe'=4,'expert'=64] {'expert'}, dimensions={0} | all-to-all | bytes 4718592 | tf_op jit(solution)/shard_map/all_to_all | solution.py:417
  167.9 6.5 %all-to-all-start.3 = ((bf16[64,16,1152]{2,1,0:T(8,128)(2,1)}), bf16[64,16,1152]{2,1,0:T(8,128)(2,1)S(1)}, u32[]{:S(2)}, u32[]{:S(2)}) async-start(bf16[64,16,1152]{2,1,0:T(8,128)(2,1)} %bitcast.20), calls=%async_computation.3 | async-start | bytes 4718592 | tf_op jit(solution)/shard_map/all_to_all | solution.py:417
  174.5 0.6 reduce.2
  175.3 1.5 fusion.6
  176.8 1.2 select_reduce_fusion.2
  178.0 0.7 copy.49
  179.4 1.5 fusion.3
  182.1 0.7 copy.52
  182.8 1.2 multiply_divide_fusion
  184.0 1.5 broadcast_divide_fusion.w
  185.4 0.8 broadcast_divide_fusion.1.w
  186.3 1.7 copy-done.10
  187.9 0.8 copy-done.21
  188.7 3.3 %shard_map.135 = bf16[64,3584]{1,0:T(8,128)(2,1)} custom-call(bf16[1024,1152]{1,0:T(8,128)(2,1)S(1)} %bitcast.64, f32[64,2]{1,0:T(8,128)S(1)} %broadcast_divide_fusion.1.w, f32[64,2]{1,0:T(8,128)S(1)} %copy-done.21, f32[2,64]{1,0:T(2,128)S(1)} %copy-done.26, bf16[64,3584]{1,0:T(8,128)(2,1)S(1)} %bitcast.67), custom_call_target="tpu_custom_call" | custom-call | bytes 1024 | tf_op jit(solution)/shard_map/pallas_call | solution.py:399
  192.0 3.1 %collective-permute-start = (bf16[1,64,3584]{2,1,0:T(8,128)(2,1)}, bf16[1,64,3584]{2,1,0:T(8,128)(2,1)}, u32[]{:S(2)}, u32[]{:S(2)}) collective-permute-start(bf16[1,64,3584]{2,1,0:T(8,128)(2,1)} %bitcast.19), channel_id=1, source_target_pairs={{0,64},{64,128},{128,192},{192,0},{1,65},{65,129},{129,193},{193,1... | collective-permute-start | bytes 1376264 | tf_op jit(solution)/shard_map/ppermute | solution.py:422
  195.1 17.2 %all-to-all-done.3 = bf16[64,16,1152]{2,1,0:T(8,128)(2,1)S(1)} async-done(((bf16[64,16,1152]{2,1,0:T(8,128)(2,1)}), bf16[64,16,1152]{2,1,0:T(8,128)(2,1)S(1)}, u32[]{:S(2)}, u32[]{:S(2)}) %all-to-all-start.3) | async-done | bytes 2359328 | tf_op jit(solution)/shard_map/all_to_all | solution.py:417
  212.3 0.8 copy-done.22
  213.1 2.6 %shard_map.136 = (f32[64,3584]{1,0:T(8,128)S(1)}, f32[64,256]{1,0:T(8,128)S(1)}) custom-call(bf16[1024,1152]{1,0:T(8,128)(2,1)S(1)} %bitcast.63, f32[64,2]{1,0:T(8,128)S(1)} %copy-done.22, f32[64,2]{1,0:T(8,128)S(1)} %copy.47.refs_3_.ids_c, f32[2,64]{1,0:T(2,128)S(1)} %copy-done.25), custom_call_target="tpu_custom_call" | custom-call | bytes 1024 | tf_op jit(solution)/shard_map/pallas_call | solution.py:399
  215.7 0.9 copy-done.19
  216.8 0.7 multiply_reduce_fusion.1
  217.5 2.0 fusion.8
  219.8 5.2 %collective-permute-start.1 = (bf16[1,64,3584]{2,1,0:T(8,128)(2,1)S(1)}, bf16[1,64,3584]{2,1,0:T(8,128)(2,1)S(1)}, u32[]{:S(2)}, u32[]{:S(2)}) collective-permute-start(bf16[1,64,3584]{2,1,0:T(8,128)(2,1)S(1)} %fusion.19), channel_id=1, source_target_pairs={{0,192},{64,0},{128,64},{192,128},{1,193},{65,1},{129,65},{193,129... | collective-permute-start | bytes 1376264 | tf_op jit(solution)/shard_map/ppermute | solution.py:422
  225.1 18.3 %collective-permute-done.1 = bf16[1,64,3584]{2,1,0:T(8,128)(2,1)S(1)} collective-permute-done((bf16[1,64,3584]{2,1,0:T(8,128)(2,1)S(1)}, bf16[1,64,3584]{2,1,0:T(8,128)(2,1)S(1)}, u32[]{:S(2)}, u32[]{:S(2)}) %collective-permute-start.1) | collective-permute-done | bytes 458784 | tf_op jit(solution)/shard_map/ppermute | solution.py:422
  243.4 1.8 copy.60
  245.2 0.8 copy.61
  (71 shorter events, 3.6 us)
Async XLA Ops:
  0.6 174.7 %copy-start = (bf16[1,3584,32]{1,2,0:T(8,128)(2,1)S(1)}, bf16[1,3584,32]{1,2,0:T(8,128)(2,1)}, u32[]{:S(2)}) copy-start(bf16[1,3584,32]{1,2,0:T(8,128)(2,1)} %param.18) | copy-start | bytes 688132
  2.1 1.0 copy-start.11
  3.1 1.0 copy-start.16
  4.2 0.7 copy-start.23
  7.2 2.2 copy-start.1
  9.4 9.5 %copy-start.30 = (s32[1,64,2]{1,2,0:T(2,128)S(1)}, s32[1,64,2]{1,2,0:T(2,128)}, u32[]{:S(2)}) copy-start(s32[1,64,2]{1,2,0:T(2,128)} %param.13) | copy-start | bytes 1540
  9.4 10.3 %copy-start.13 = (bf16[1,64,3584]{2,1,0:T(8,128)(2,1)S(1)}, bf16[1,64,3584]{2,1,0:T(8,128)(2,1)}, u32[]{:S(2)}) copy-start(bf16[1,64,3584]{2,1,0:T(8,128)(2,1)} %param.12) | copy-start | bytes 1376260
  9.4 10.3 %copy-start.24 = (f32[1,3584]{1,0:T(1,128)S(1)}, f32[1,3584]{1,0:T(1,128)}, u32[]{:S(2)}) copy-start(f32[1,3584]{1,0:T(1,128)} %refs_1_.1) | copy-start | bytes 43012
  9.4 67.8 %all-to-all-start.1 = ((bf16[64,16,2304]{2,1,0:T(8,128)(2,1)}), bf16[64,16,2304]{2,1,0:T(8,128)(2,1)}, u32[]{:S(2)}, u32[]{:S(2)}) async-start(bf16[64,16,2304]{2,1,0:T(8,128)(2,1)} %bitcast.53), calls=%async_computation.1 | async-start | bytes 9437184 | tf_op jit(solution)/shard_map/all_to_all | solution.py:417
  19.6 4.3 %copy-start.20 = (f32[64,2]{1,0:T(8,128)}, f32[64,2]{1,0:T(8,128)S(1)}, u32[]{:S(2)}) copy-start(f32[64,2]{1,0:T(8,128)S(1)} %copy.48.refs_2_.ids_c) | copy-start | bytes 1540
  19.7 2.3 copy-start.2
  23.9 1.4 copy-start.9
  77.2 7.0 %copy-start.18 = (bf16[640,256]{1,0:T(8,128)(2,1)S(1)}, bf16[640,256]{1,0:T(8,128)(2,1)}, u32[]{:S(2)}) copy-start(bf16[640,256]{1,0:T(8,128)(2,1)} %constant.21.clone.gather) | copy-start | bytes 983044
  77.2 37.9 %all-to-all-start = ((bf16[64,16,1152]{2,1,0:T(8,128)(2,1)}), bf16[64,16,1152]{2,1,0:T(8,128)(2,1)S(1)}, u32[]{:S(2)}, u32[]{:S(2)}) async-start(bf16[64,16,1152]{2,1,0:T(8,128)(2,1)} %bitcast.62), calls=%async_computation | async-start | bytes 4718592 | tf_op jit(solution)/shard_map/all_to_all | solution.py:417
  84.3 2.0 copy-start.3
  86.3 2.0 copy-start.5
  88.3 2.0 copy-start.7
  90.4 1.2 copy-start.14
  115.1 2.0 copy-start.4
  117.2 2.0 copy-start.6
  119.2 2.0 copy-start.8
  121.2 1.2 copy-start.15
  167.9 10.8 %copy-start.12 = (bf16[1,64,3584]{2,1,0:T(8,128)(2,1)S(1)}, bf16[1,64,3584]{2,1,0:T(8,128)(2,1)}, u32[]{:S(2)}) copy-start(bf16[1,64,3584]{2,1,0:T(8,128)(2,1)} %param.14) | copy-start | bytes 1376260
  167.9 44.4 %all-to-all-start.3 = ((bf16[64,16,1152]{2,1,0:T(8,128)(2,1)}), bf16[64,16,1152]{2,1,0:T(8,128)(2,1)S(1)}, u32[]{:S(2)}, u32[]{:S(2)}) async-start(bf16[64,16,1152]{2,1,0:T(8,128)(2,1)} %bitcast.20), calls=%async_computation.3 | async-start | bytes 4718592 | tf_op jit(solution)/shard_map/all_to_all | solution.py:417
  175.1 6.4 %copy-start.28 = (s32[1,64,2]{1,2,0:T(2,128)S(1)}, s32[1,64,2]{1,2,0:T(2,128)}, u32[]{:S(2)}) copy-start(s32[1,64,2]{1,2,0:T(2,128)} %param.16) | copy-start | bytes 1540
  175.1 11.2 %copy-start.26 = (f32[2,64]{1,0:T(2,128)S(1)}, f32[2,64]{1,0:T(2,128)}, u32[]{:S(2)}) copy-start(f32[2,64]{1,0:T(2,128)} %get-tuple-element.14.ids_r) | copy-start | bytes 1540
  178.9 0.5 copy-start.31
  179.4 32.9 %copy-start.25 = (f32[2,64]{1,0:T(2,128)S(1)}, f32[2,64]{1,0:T(2,128)}, u32[]{:S(2)}) copy-start(f32[2,64]{1,0:T(2,128)} %get-tuple-element.12.ids_r) | copy-start | bytes 1540
  179.4 2.6 %copy-start.33 = (f32[64]{0:T(128)}, f32[64]{0:T(128)S(1)}, u32[]{:S(2)}) copy-start(f32[64]{0:T(128)S(1)} %fusion.30) | copy-start | bytes 772
  180.9 0.6 copy-start.27
  186.3 1.7 copy-start.10
  187.9 0.8 copy-start.21
  192.0 25.5 %copy-start.29 = (f32[64]{0:T(128)S(1)}, f32[64]{0:T(128)}, u32[]{:S(2)}) copy-start(f32[64]{0:T(128)} %get-tuple-element.6) | copy-start | bytes 772
  192.0 33.0 %collective-permute-start = (bf16[1,64,3584]{2,1,0:T(8,128)(2,1)}, bf16[1,64,3584]{2,1,0:T(8,128)(2,1)}, u32[]{:S(2)}, u32[]{:S(2)}) collective-permute-start(bf16[1,64,3584]{2,1,0:T(8,128)(2,1)} %bitcast.19), channel_id=1, source_target_pairs={{0,64},{64,128},{128,192},{192,0},{1,65},{65,129},{129,193},{193,1... | collective-permute-start | bytes 1376264 | tf_op jit(solution)/shard_map/ppermute | solution.py:422
  212.3 0.8 copy-start.22
  213.1 6.5 %copy-start.17 = (bf16[1,64,3584]{2,1,0:T(8,128)(2,1)S(1)}, bf16[1,64,3584]{2,1,0:T(8,128)(2,1)}, u32[]{:S(2)}) copy-start(bf16[1,64,3584]{2,1,0:T(8,128)(2,1)} %param.15) | copy-start | bytes 1376260
  215.7 0.9 copy-start.19
  216.6 2.9 %copy-start.32 = (f32[64]{0:T(128)S(1)}, f32[64]{0:T(128)}, u32[]{:S(2)}) copy-start(f32[64]{0:T(128)} %copy-done.31) | copy-start | bytes 772
  216.6 2.9 %copy-start.34 = (f32[64]{0:T(128)S(1)}, f32[64]{0:T(128)}, u32[]{:S(2)}) copy-start(f32[64]{0:T(128)} %copy-done.33) | copy-start | bytes 772
  219.8 23.5 %collective-permute-start.1 = (bf16[1,64,3584]{2,1,0:T(8,128)(2,1)S(1)}, bf16[1,64,3584]{2,1,0:T(8,128)(2,1)S(1)}, u32[]{:S(2)}, u32[]{:S(2)}) collective-permute-start(bf16[1,64,3584]{2,1,0:T(8,128)(2,1)S(1)} %fusion.19), channel_id=1, source_target_pairs={{0,192},{64,0},{128,64},{192,128},{1,193},{65,1},{129,65},{193,129... | collective-permute-start | bytes 1376264 | tf_op jit(solution)/shard_map/ppermute | solution.py:422
where the time goes:
time: 247 us; the launch traced here: 246 us
  waiting for transfers between devices  93.6 us (38%)
  Pallas kernels  36.7 us (15%)
  blocking collectives  36.3 us (15%)
  local copies, waits for them, and re-layouts  32.9 us (13%)
  starting transfers between devices  31.3 us (13%)
  other arithmetic  9.31 us (4%)
  matrix products  4.95 us (2%)
    all_to_all x3, waiting for transfers between devices, swapped(): return lax.all_to_all(chunks, 'expert', 0, 0, tiled=True).reshape(shape)  75.3 us
    all_to_all x1, blocking collectives, swapped(): return lax.all_to_all(chunks, 'expert', 0, 0, tiled=True).reshape(shape)  36.3 us
    unnamed x72, local copies, waits for them, and re-layouts  31.1 us
    all_to_all x3, starting transfers between devices, swapped(): return lax.all_to_all(chunks, 'expert', 0, 0, tiled=True).reshape(shape)  23 us
    ppermute x2, waiting for transfers between devices, passed_along(): return lax.ppermute(x, axis, [(i, (i + by) % n) for i in range(n)])  18.3 us
    pallas_call x1, Pallas kernels, expert_backward(): pl.pallas_call(kernel, out_shape=jax.ShapeDtypeStruct((chunks.shape[0], L...  17.4 us
    pallas_call x1, Pallas kernels, expert_forward(): pl.pallas_call(kernel, out_shape=jax.ShapeDtypeStruct(chunks.shape, jnp.b...  9.17 us
    ppermute x2, starting transfers between devices, passed_along(): return lax.ppermute(x, axis, [(i, (i + by) % n) for i in range(n)])  8.27 us
  transfers between devices with their start and end apart: 5, of which 4 were waited for; matrix products, arithmetic and copies ran while one was open for 6% of the time, Pallas kernels for 10%

commit v1 on v0

v1 whole, which is shorter than its diff:
```python
import jax
import jax.numpy as jnp
import numpy as np
from jax import lax
from jax.experimental import pallas as pl
from jax.experimental.pallas import tpu as pltpu
from jax.sharding import PartitionSpec as P

epsilon = 1e-06
VMEM_LIMIT = 60 * 1024 * 1024
CAP = 5
LANES = 1152
ROWS = 16
TAIL = 3 * LANES
FAR = pl.BlockSpec(memory_space=pltpu.HBM)
NEAR = pl.BlockSpec(memory_space=pltpu.VMEM)


def selections():
    body = np.zeros((3, 16, CAP, 16, ROWS), np.float32)
    tail = np.zeros((CAP, 16, CAP, 16, ROWS), np.float32)
    for i in range(16):
        for s in range(CAP):
            tail[s, i, s, i, 15] = 1
            for g in range(3):
                body[g, i, s, i, 5 * g + s] = 1
    body, tail = body.reshape(240, 256), tail.reshape(400, 256)
    gather = np.concatenate([body, tail])
    scatter = np.concatenate([body.T] + [tail[80 * s : 80 * s + 80].T for s in range(CAP)], axis=1)
    scatter = np.concatenate([scatter, tail.reshape(CAP, 80, 256).sum(0).T], axis=1)
    blocks = [scatter[:, :240]] + [scatter[:, 240 + 80 * n : 320 + 80 * n] for n in range(CAP + 1)]
    scatter = np.concatenate([np.pad(b, ((0, 0), (0, 240 - b.shape[1]))) for b in blocks])
    return jnp.asarray(gather, jnp.bfloat16), jnp.asarray(scatter, jnp.bfloat16)


def params():
    return dict(
        compiler_params=pltpu.CompilerParams(vmem_limit_bytes=VMEM_LIMIT),
        cost_estimate=pl.CostEstimate(flops=0, bytes_accessed=1024, transcendentals=0),
    )


def f32(x):
    return x.astype(jnp.float32)


def count(hits, axis):
    return jnp.sum(jnp.where(hits, 1.0, 0.0), axis=axis, keepdims=True)


def place_of(position):
    expert = lax.bitwise_and(lax.shift_right_logical(position, 4), 31)
    row = lax.bitwise_and(position, 15)
    block = jnp.where(row >= 5, 1, 0) + jnp.where(row >= 10, 1, 0) + jnp.where(row >= 15, 1, 0)
    return expert, row, block, row - 5 * block


def as_row(column, copies):
    n = column.shape[0]
    shape = (n, copies * n)
    lane = lax.bitwise_and(lax.broadcasted_iota(jnp.int32, shape, 1), n - 1)
    hit = lax.broadcasted_iota(jnp.int32, shape, 0) == lane
    return jnp.sum(jnp.where(hit, column, 0.0), axis=0, keepdims=True)


def pack(units, gain, routes):
    n, m = len(units), len(routes)
    tokens, width = units[0][0].shape
    half_rows = 32 * ROWS
    operands = [*routes, gain, *[rows for rows, _, _ in units]]

    def kernel(*refs):
        far, out = refs[: n + m + 1], refs[n + m + 1]
        near = refs[n + m + 2 : 2 * (n + m) + 3]
        made, low, high, sems = refs[2 * (n + m) + 3 :]
        loads = [
            pltpu.make_async_copy(src, dst, sems.at[i]) for i, (src, dst) in enumerate(zip(far, near))
        ]
        for load in loads:
            load.start()
        for load in loads[: m + 1]:
            load.wait()
        gain_ref = near[m]
        shape = (half_rows, 2 * tokens)
        expert, row, block, slot = place_of(lax.broadcasted_iota(jnp.int32, shape, 0))
        right = lax.broadcasted_iota(jnp.int32, shape, 1) >= tokens
        stores = []
        for route in range(m):
            ids = f32(near[route][...])
            first, second = ids[:, 0:1], ids[:, 1:2]
            first_r, second_r = as_row(first, 2), as_row(second, 2)
            square = (tokens, 2 * tokens)
            lane = lax.bitwise_and(lax.broadcasted_iota(jnp.int32, square, 1), tokens - 1)
            before = lax.broadcasted_iota(jnp.int32, square, 0) < lane
            slot_0 = count((first == first_r) & before, 0)
            slot_1 = count(first == second_r, 0) + count((second == second_r) & before, 0)
            key_0, key_1 = first_r * 8 + slot_0, second_r * 8 + slot_1

            def hits(key, key_0=key_0, key_1=key_1):
                key = f32(key)
                return (key_0 == key) | (key_1 == key)

            def matrix(mask):
                return jnp.where(mask, 1.0, 0.0).astype(jnp.bfloat16)

            own = hits(expert * 8 + slot)
            pick_low = matrix(own & (block == jnp.where(right, 1, 0)))
            third = own & (block == 2) & ~right
            pick_rest = matrix(third)
            picks = [
                matrix(third | (hits(expert * 8 + s) & (row == 15) & right)) for s in range(CAP)
            ]
            for u in range(n):
                if units[u][2] != route:
                    continue
                loads[m + 1 + u].wait()
                x = near[m + 1 + u][...]
                if units[u][1]:
                    v = f32(x)
                    inverse = lax.rsqrt(jnp.mean(v * v, axis=-1, keepdims=True) + epsilon)
                    x = (v * inverse * gain_ref[...]).astype(jnp.bfloat16)
                low[0:tokens, :] = x[:, :LANES]
                low[tokens:, :] = x[:, LANES : 2 * LANES]
                high[0:tokens, :] = x[:, 2 * LANES : TAIL]
                high[tokens:, :] = jnp.zeros((tokens, LANES), jnp.bfloat16)
                for s in range(CAP):
                    high[tokens:, 128 * s : 128 * s + 128] = x[:, TAIL:]
                for s in range(9):
                    cols = slice(128 * s, 128 * s + 128)
                    part = jnp.dot(pick_low, low[:, cols], preferred_element_type=jnp.float32)
                    part += jnp.dot(
                        picks[s] if s < CAP else pick_rest,
                        high[:, cols],
                        preferred_element_type=jnp.float32,
                    )
                    made[:, u * LANES + 128 * s : u * LANES + 128 * s + 128] = part.astype(
                        jnp.bfloat16
                    )
                lanes = pl.ds(u * LANES, LANES)
                for r in range(2):
                    stores.append(
                        pltpu.make_async_copy(
                            made.at[:, lanes],
                            out.at[pl.ds(half_rows * r, half_rows), lanes],
                            sems.at[n + m + 1 + 2 * u + r],
                        )
                    )
                    stores[-1].start()
        for store in stores:
            store.wait()

    return pl.pallas_call(
        kernel,
        out_shape=jax.ShapeDtypeStruct((2 * half_rows, n * LANES), jnp.bfloat16),
        in_specs=[FAR] * (n + m + 1),
        out_specs=FAR,
        scratch_shapes=[pltpu.VMEM(v.shape, v.dtype) for v in operands]
        + [
            pltpu.VMEM((half_rows, n * LANES), jnp.bfloat16),
            pltpu.VMEM((2 * tokens, LANES), jnp.bfloat16),
            pltpu.VMEM((2 * tokens, LANES), jnp.bfloat16),
            pltpu.SemaphoreType.DMA((3 * n + m + 1,)),
        ],
        **params(),
    )(*operands)


def unpack(chunks, gather, x, offset, start):
    def step(b, carry):
        held = pl.ds(pl.multiple_of(256 * b, 256), 256)
        rows = pl.ds(pl.multiple_of(start + 80 * b, 16), 80)
        for c in range(3):
            part = jnp.dot(
                gather[:240, :],
                chunks[held, offset + 384 * c : offset + 384 * c + 384],
                preferred_element_type=jnp.float32,
            ).astype(jnp.bfloat16)
            for g in range(3):
                at = g * LANES + 384 * c
                x[rows, at : at + 384] = part[80 * g : 80 * g + 80]
        total = jnp.zeros((80, 128), jnp.float32)
        for s in range(CAP):
            total += jnp.dot(
                gather[240 + 80 * s : 320 + 80 * s, :],
                chunks[held, offset + 128 * s : offset + 128 * s + 128],
                preferred_element_type=jnp.float32,
            )
        x[rows, TAIL : TAIL + 128] = total.astype(jnp.bfloat16)
        return carry

    lax.fori_loop(0, 4, step, 0)


def repack(chunks, offset, scatter, made, rest, extra=None):
    def step(b, carry):
        held = pl.ds(pl.multiple_of(256 * b, 256), 256)
        stacked = pl.ds(pl.multiple_of(240 * b, 16), 240)
        rows = pl.ds(pl.multiple_of(80 * b, 16), 80)
        for s in range(9):
            cols = slice(128 * s, 128 * s + 128)
            part = jnp.dot(scatter[:256, :], made[stacked, cols], preferred_element_type=jnp.float32)
            source = rest if s < CAP else extra if s == CAP else None
            if source is not None:
                part += jnp.dot(
                    scatter[256 + 256 * s : 512 + 256 * s, :80],
                    source[rows, :],
                    preferred_element_type=jnp.float32,
                )
            chunks[held, offset + 128 * s : offset + 128 * s + 128] = part.astype(jnp.bfloat16)
        return carry

    lax.fori_loop(0, 4, step, 0)


def put_result(made, rest, product):
    def step(c, carry):
        for g in range(3):
            cols = pl.ds(pl.multiple_of(g * LANES + 384 * c, 128), 384)
            part = product(cols).astype(jnp.bfloat16)
            at = pl.ds(pl.multiple_of(384 * c, 128), 384)
            for b in range(4):
                made[240 * b + 80 * g : 240 * b + 80 * g + 80, at] = part[80 * b : 80 * b + 80]
        return carry

    lax.fori_loop(0, 3, step, 0)
    rest[...] = product(pl.ds(TAIL, 128)).astype(jnp.bfloat16)


def experts(chunks, tables, weights):
    width, units = weights[0].shape
    contract = (((1,), (1,)), ((), ()))
    operands = [*tables, *weights]

    def kernel(far, *refs):
        far_in, far_out = refs[:5], refs[5]
        near, gather, scatter, wg, wu, wd, x, cot, hidden, d_gate, d_up, made, rest, extra, sems = (
            refs[6:]
        )
        lanes = [pl.ds(u * LANES, LANES) for u in range(3)]
        parts = [
            pltpu.make_async_copy(far.at[:, lanes[u]], near.at[:, lanes[u]], sems.at[u])
            for u in range(3)
        ]
        tables_in = [
            pltpu.make_async_copy(src, dst, sems.at[3 + n])
            for n, (src, dst) in enumerate(zip(far_in, (gather, scatter, wg, wu, wd)))
        ]
        for load in (tables_in[0], parts[0], parts[2], *tables_in[2:4], parts[1], tables_in[4], tables_in[1]):
            load.start()
        tables_in[0].wait()
        parts[0].wait()
        unpack(near, gather, x, 0, 0)
        parts[2].wait()
        unpack(near, gather, x, 2 * LANES, 320)
        parts[1].wait()
        unpack(near, gather, cot, LANES, 0)
        for load in tables_in[1:]:
            load.wait()

        def first(k, inner):
            cols = pl.ds(pl.multiple_of(k * 256, 256), 256)
            gate = jnp.dot(x[...], wg[:, cols], preferred_element_type=jnp.float32)
            upper = jnp.dot(x[...], wu[:, cols], preferred_element_type=jnp.float32)
            s = jax.nn.sigmoid(gate)
            active = gate * s
            value = (active * upper).astype(jnp.bfloat16)
            hidden[:, cols] = value[320:]
            d_hidden = lax.dot_general(
                cot[...], wd[cols, :], contract, preferred_element_type=jnp.float32
            )
            gate, upper, s, active = gate[:320], upper[:320], s[:320], active[:320]
            d_gate[:, cols] = (d_hidden * upper * s * (1.0 + gate * (1.0 - s))).astype(
                jnp.bfloat16
            )
            d_up[:, cols] = (d_hidden * active).astype(jnp.bfloat16)
            return inner + jnp.sum(f32(value[:320]) * d_hidden, axis=1, keepdims=True)

        inner = lax.fori_loop(0, units // 256, first, jnp.zeros((320, 1), jnp.float32))
        slot = lax.rem(lax.broadcasted_iota(jnp.int32, (320, 128), 0), CAP)
        lane = lax.broadcasted_iota(jnp.int32, (320, 128), 1)
        extra[...] = jnp.where(slot == lane, inner, 0.0).astype(jnp.bfloat16)

        def back(cols):
            return lax.dot_general(
                d_gate[...], wg[cols, :], contract, preferred_element_type=jnp.float32
            ) + lax.dot_general(
                d_up[...], wu[cols, :], contract, preferred_element_type=jnp.float32
            )

        def outward(cols):
            return jnp.dot(hidden[...], wd[:, cols], preferred_element_type=jnp.float32)

        stores = [
            pltpu.make_async_copy(
                near.at[:, lanes[u]], far_out.at[:, lanes[u]], sems.at[8 + u]
            )
            for u in range(2)
        ]
        put_result(made, rest, back)
        repack(near, 0, scatter, made, rest, extra)
        stores[0].start()
        put_result(made, rest, outward)
        repack(near, LANES, scatter, made, rest)
        stores[1].start()
        for store in stores:
            store.wait()

    return pl.pallas_call(
        kernel,
        out_shape=jax.ShapeDtypeStruct((chunks.shape[0], 2 * LANES), jnp.bfloat16),
        in_specs=[FAR] * 6,
        out_specs=FAR,
        scratch_shapes=[pltpu.VMEM(v.shape, v.dtype) for v in (chunks, *operands)]
        + [
            pltpu.VMEM((640, width), jnp.bfloat16),
            pltpu.VMEM((320, width), jnp.bfloat16),
            pltpu.VMEM((320, units), jnp.bfloat16),
            pltpu.VMEM((320, units), jnp.bfloat16),
            pltpu.VMEM((320, units), jnp.bfloat16),
            pltpu.VMEM((960, LANES), jnp.bfloat16),
            pltpu.VMEM((320, 128), jnp.bfloat16),
            pltpu.VMEM((320, 128), jnp.bfloat16),
            pltpu.SemaphoreType.DMA((10,)),
        ],
        **params(),
    )(chunks, *operands)


def spread_weights(weights, routes):
    tokens = routes[0].shape[0]
    total_rows = 64 * ROWS
    n = len(routes)

    def kernel(*refs):
        w_refs, id_refs, outs = refs[:n], refs[n : 2 * n], refs[2 * n :]
        square = (tokens, tokens)
        before = lax.broadcasted_iota(jnp.int32, square, 1) < lax.broadcasted_iota(
            jnp.int32, square, 0
        )
        shape = (tokens, total_rows)
        expert, row, block, slot = place_of(lax.broadcasted_iota(jnp.int32, shape, 1))
        for at in range(n):
            w, ids = w_refs[at], f32(id_refs[at][...])
            first, second = ids[:, 0:1], ids[:, 1:2]
            first_r, second_r = as_row(first, 1), as_row(second, 1)
            slot_0 = count((first == first_r) & before, 1)
            slot_1 = count(second == first_r, 1) + count((second == second_r) & before, 1)
            key_0, key_1 = first * 8 + slot_0, second * 8 + slot_1

            def spread(key, w=w, key_0=key_0, key_1=key_1):
                key = f32(key)
                total = jnp.where(key_0 == key, w[:, 0:1], 0.0) + jnp.where(
                    key_1 == key, w[:, 1:2], 0.0
                )
                upper = f32(total.astype(jnp.bfloat16))
                return upper, total - upper

            def put(ref, start, values, mask):
                for i, value in enumerate(values):
                    ref[start + tokens * i : start + tokens * i + tokens, :] = jnp.where(
                        mask, value, 0.0
                    ).astype(jnp.bfloat16)

            values = spread(expert * 8 + slot)
            for g in range(3):
                put(outs[2 * at], 2 * tokens * g, values, block == g)
            for s in range(CAP):
                put(outs[2 * at + 1], 2 * tokens * s, spread(expert * 8 + s), row == 15)
            if at == n - 1:
                for k, (chosen, number) in enumerate(((first, slot_0), (second, slot_1))):
                    outs[2 * n][tokens * k : tokens * k + tokens, :] = jnp.where(
                        (row == 15) & (f32(expert) == chosen), 1.0, 0.0
                    ).astype(jnp.bfloat16)
                    outs[2 * n + 1][:, 128 * k : 128 * k + 128] = jnp.broadcast_to(
                        number, (tokens, 128)
                    )

    shapes = [(6 * tokens, total_rows), (2 * CAP * tokens, total_rows)] * n
    shapes.append((2 * tokens, total_rows))
    return pl.pallas_call(
        kernel,
        out_shape=[jax.ShapeDtypeStruct(shape, jnp.bfloat16) for shape in shapes]
        + [jax.ShapeDtypeStruct((tokens, 256), jnp.float32)],
        in_specs=[NEAR] * (2 * n),
        out_specs=[NEAR] * (2 * n + 2),
        **params(),
    )(*weights, *routes)


def finish(chunks, spreads, rows, routes, picked, gain, router_rows):
    forward, saved, cotangent = rows
    tokens, width = forward.shape
    operands = [*spreads, forward, saved, cotangent, routes, picked, gain, router_rows]
    n = len(operands)

    def kernel(far, *refs):
        far_in, out_f, out_b = refs[:n], refs[n], refs[n + 1]
        held = refs[n + 4 : 2 * n + 4]
        result, gradient = refs[n + 2], refs[n + 3]
        near, total, sems = refs[2 * n + 4 :]
        parts_f, tails_f, parts_b, tails_b, picks, slots = held[:6]
        v_f, v_b, cot, ids, chosen, gain_ref, router_ref = held[6:]
        lanes = [pl.ds(u * LANES, LANES) for u in range(2)]
        chunk_loads = [
            pltpu.make_async_copy(far.at[:, lanes[u]], near.at[:, lanes[u]], sems.at[n + u])
            for u in range(2)
        ]
        loads = [
            pltpu.make_async_copy(src, dst, sems.at[i])
            for i, (src, dst) in enumerate(zip(far_in, held))
        ]
        order = [2, 3, 4, 5, 7, 8, 9, 10, 11, 12, 0, 1, 6]
        chunk_loads[0].start()
        for i in order[:10]:
            loads[i].start()
        chunk_loads[1].start()
        for i in order[10:]:
            loads[i].start()

        def add_up(offset, parts, tails, store):
            for c in range(3):
                at = offset + 384 * c
                part = jnp.dot(
                    parts[...], near[:, at : at + 384], preferred_element_type=jnp.float32
                )
                for g in range(3):
                    at = 2 * tokens * g
                    store(
                        g * LANES + 384 * c,
                        384,
                        part[at : at + tokens] + part[at + tokens : at + 2 * tokens],
                    )
            rest = jnp.zeros((2 * tokens, 128), jnp.float32)
            for s in range(CAP):
                rest += jnp.dot(
                    tails[2 * tokens * s : 2 * tokens * (s + 1), :],
                    near[:, offset + 128 * s : offset + 128 * s + 128],
                    preferred_element_type=jnp.float32,
                )
            store(TAIL, 128, rest[:tokens] + rest[tokens:])

        chunk_loads[0].wait()
        for i in order[:10]:
            loads[i].wait()
        found = jnp.dot(picks[...], near[:, 640:768], preferred_element_type=jnp.float32)
        lane = f32(lax.broadcasted_iota(jnp.int32, (tokens, 128), 1))
        inner = [
            jnp.sum(
                jnp.where(
                    lane == slots[:, 128 * k : 128 * k + 128],
                    found[tokens * k : tokens * k + tokens],
                    0.0,
                ),
                axis=1,
                keepdims=True,
            )
            for k in range(2)
        ]
        scores = [chosen[:, k : k + 1] for k in range(2)]
        whole = scores[0] + scores[1]
        mean = (inner[0] * scores[0] + inner[1] * scores[1]) / whole
        numbers = f32(ids[...])
        d_logits = jnp.zeros((tokens, 128), jnp.float32)
        for k in range(2):
            d_logit = (inner[k] - mean) / whole * scores[k] * (1.0 - scores[k])
            d_logits += jnp.where(lane == numbers[:, k : k + 1], d_logit, 0.0)
        pieces, left = [], d_logits
        for _ in range(3):
            pieces.append(left.astype(jnp.bfloat16))
            left = left - f32(pieces[-1])

        def keep(at, size, value):
            for piece in pieces:
                value += jnp.dot(
                    piece, router_ref[:, at : at + size], preferred_element_type=jnp.float32
                )
            total[:, at : at + size] = value

        add_up(0, parts_b, tails_b, keep)
        v = f32(v_b[...])
        inverse = lax.rsqrt(jnp.mean(v * v, axis=-1, keepdims=True) + epsilon)
        scaled = total[...] * gain_ref[...]
        projected = jnp.mean(v * scaled, axis=-1, keepdims=True)
        d_rows = scaled * inverse - v * (inverse * inverse * inverse * projected)
        gradient[...] = (f32(cot[...]) + d_rows).astype(jnp.bfloat16)
        stores = [
            pltpu.make_async_copy(gradient, out_b, sems.at[n + 2]),
            pltpu.make_async_copy(result, out_f, sems.at[n + 3]),
        ]
        stores[0].start()
        chunk_loads[1].wait()
        for i in order[10:]:
            loads[i].wait()

        def put(at, size, value):
            result[:, at : at + size] = (f32(v_f[:, at : at + size]) + value).astype(jnp.bfloat16)

        add_up(LANES, parts_f, tails_f, put)
        stores[1].start()
        for store in stores:
            store.wait()

    row = jax.ShapeDtypeStruct((tokens, width), jnp.bfloat16)
    return pl.pallas_call(
        kernel,
        out_shape=[row, row],
        in_specs=[FAR] * (n + 1),
        out_specs=[FAR] * 2,
        scratch_shapes=[pltpu.VMEM((tokens, width), jnp.bfloat16)] * 2
        + [pltpu.VMEM(v.shape, v.dtype) for v in operands]
        + [
            pltpu.VMEM(chunks.shape, jnp.bfloat16),
            pltpu.VMEM((tokens, width), jnp.float32),
            pltpu.SemaphoreType.DMA((n + 4,)),
        ],
        **params(),
    )(chunks, *operands)


def swapped(chunks):
    shape = chunks.shape
    chunks = chunks.reshape(shape[0] // ROWS, ROWS, shape[1])
    return lax.all_to_all(chunks, "expert", 0, 0, tiled=True).reshape(shape)


def passed_along(x, axis, by):
    n = lax.axis_size(axis)
    return lax.ppermute(x, axis, [(i, (i + by) % n) for i in range(n)])


def normalise(values, gain_row):
    inverse = lax.rsqrt(jnp.mean(values * values, axis=-1, keepdims=True) + epsilon)
    return values * inverse * gain_row


def picked_scores(values, gain_row, router_map, routes):
    normed = normalise(values.astype(jnp.float32), gain_row)
    logits = jnp.dot(normed, router_map.astype(jnp.float32), precision=lax.Precision.HIGHEST)
    scores = jax.nn.sigmoid(logits)
    choices_axis = jnp.arange(router_map.shape[1], dtype=jnp.int32)
    onehot = (routes[:, :, None] == choices_axis[None, None, :]).astype(scores.dtype)
    return jnp.sum(onehot * scores[:, None, :], axis=-1)


def body(
    forward_rows,
    forward_routes,
    saved_rows,
    cotangent,
    backward_routes,
    norm_gain,
    router,
    gate_weight,
    up_weight,
    down_weight,
):
    gain_row, router_map = norm_gain[0], router[0]
    weights = (gate_weight[0, 0], up_weight[0, 0], down_weight[0, 0])
    tables = selections()
    backward_ids, forward_ids = backward_routes[0], forward_routes[0]

    saved, cotan, forward = saved_rows[0], cotangent[0], forward_rows[0]

    sent = pack(
        [(saved, True, 0), (cotan, False, 0), (forward, True, 1)],
        norm_gain,
        [backward_ids, forward_ids],
    )
    received = swapped(sent)
    backward_scores = picked_scores(saved, gain_row, router_map, backward_ids)
    forward_scores = picked_scores(forward, gain_row, router_map, forward_ids)
    spreads = spread_weights(
        [v / jnp.sum(v, axis=1, keepdims=True) for v in (forward_scores, backward_scores)],
        [forward_ids, backward_ids],
    )
    returned = swapped(experts(received, tables, weights))
    router_rows = jnp.pad(router_map.T, ((0, 128 - router_map.shape[1]), (0, 0)))
    result, gradient = finish(
        returned, spreads, (forward, saved, cotan), backward_ids, backward_scores, norm_gain, router_rows
    )
    backward_next = passed_along(gradient[None], "pipe", -1)
    forward_next = passed_along(result[None], "pipe", 1)
    return (forward_next, backward_next)


def solution(mesh):
    in_specs = (
        P("pipe", "expert", None),
        P("pipe", "expert", None),
        P("pipe", "expert", None),
        P("pipe", "expert", None),
        P("pipe", "expert", None),
        P("pipe", None),
        P("pipe", None, None),
        P("pipe", "expert", None, None),
        P("pipe", "expert", None, None),
        P("pipe", "expert", None, None),
    )
    out_specs = (P("pipe", "expert", None), P("pipe", "expert", None))
    return jax.shard_map(body, mesh=mesh, in_specs=in_specs, out_specs=out_specs, check_vma=False)
```

time: 247 us -> 231 us (0.935)
  the two profiles are of different devices: /device:TPU:41 before, /device:TPU:1 now
where the time goes in v1:
time: 231 us; the launch traced here: 230 us
  blocking collectives  93 us (40%)
  waiting for transfers between devices  73.5 us (32%)
  Pallas kernels  44 us (19%)
  starting transfers between devices  10.9 us (5%)
  local copies, waits for them, and re-layouts  5.53 us (2%)
    all_to_all x1, blocking collectives, swapped(): return lax.all_to_all(chunks, 'expert', 0, 0, tiled=True).reshape(shape)  93 us
    all_to_all x1, waiting for transfers between devices, swapped(): return lax.all_to_all(chunks, 'expert', 0, 0, tiled=True).reshape(shape)  52.1 us
    pallas_call x1, Pallas kernels, experts(): pl.pallas_call(kernel, out_shape=jax.ShapeDtypeStruct((chunks.shape[0], 2...  25.6 us
    ppermute x2, waiting for transfers between devices, passed_along(): return lax.ppermute(x, axis, [(i, (i + by) % n) for i in range(n)])  21.3 us
    pallas_call x1, Pallas kernels, finish(): pl.pallas_call(kernel, out_shape=[row, row], in_specs=[FAR] * (n + 1), ou...  8.25 us
    pallas_call x1, Pallas kernels, pack(): pl.pallas_call(kernel, out_shape=jax.ShapeDtypeStruct((2 * half_rows, n *...  6.21 us
    all_to_all x1, starting transfers between devices, swapped(): return lax.all_to_all(chunks, 'expert', 0, 0, tiled=True).reshape(shape)  5.63 us
    ppermute x2, starting transfers between devices, passed_along(): return lax.ppermute(x, axis, [(i, (i + by) % n) for i in range(n)])  5.29 us
  transfers between devices with their start and end apart: 3, of which 3 were waited for; matrix products, arithmetic and copies ran while one was open for 2% of the time, Pallas kernels for 2%

profile of v1, /device:TPU:1, one launch (start us, length us, event | category | flops | bytes accessed | tf_op | source)
XLA Modules:
  0.0 230.5 jit_solution(7980100879038979920)
XLA Ops:
  0.6 1.4 copy.31.refs_0_.refs_3_.refs_9_
  2.0 1.4 copy.32.refs_1_.refs_2_
  3.4 6.2 %shard_map.131 = bf16[1024,3456]{1,0:T(8,128)(2,1)} custom-call(s32[64,2]{1,0:T(8,128)} %copy.31.refs_0_.refs_3_.refs_9_, s32[64,2]{1,0:T(8,128)} %copy.32.refs_1_.refs_2_, f32[1,3584]{1,0:T(1,128)} %refs_11_.1, bf16[64,3584]{1,0:T(8,128)(2,1)} %bitcast.32, bf16[64,3584]{1,0:T(8,128)(2,1)} %bitcast.39, bf16[64,3584]{1,0:T(8,128)(2,1)} %bitcast.34), custom_call_target="tpu_custom_call" | custom-call | bytes 1024 | tf_op jit(solution)/shard_map/pallas_call | solution.py:152
  9.6 93.0 %all_to_all.10 = bf16[64,16,3456]{2,1,0:T(8,128)(2,1)} all-to-all(bf16[64,16,3456]{2,1,0:T(8,128)(2,1)} %bitcast.30), channel_id=1, replica_groups=mesh['pipe'=4,'expert'=64] {'expert'}, dimensions={0} | all-to-all | bytes 14155776 | tf_op jit(solution)/shard_map/all_to_all | solution.py:523
  102.6 25.6 %shard_map.132 = bf16[1024,2304]{1,0:T(8,128)(2,1)} custom-call(bf16[1024,3456]{1,0:T(8,128)(2,1)} %bitcast.29, bf16[640,256]{1,0:T(8,128)(2,1)} %constant.19.clone.refs_0_, bf16[1792,240]{1,0:T(8,128)(2,1)} %constant.20.clone.refs_1_, bf16[3584,512]{1,0:T(8,128)(2,1)} %bitcast.36, bf16[3584,512]{1,0:T(8,128)(2,1)} %bitcast.37, bf16[512,3584]{1,0:T(8,128)(2,1)} %bitcast.38), custom_call_target="tpu_custom_call" | custom-call | bytes 1024 | tf_op jit(solution)/shard_map/pallas_call | solution.py:308
  128.3 0.0 copy-start.4
  128.3 0.0 copy-start
  128.3 0.0 copy-start.3
  128.3 0.0 copy-start.5
  128.3 0.0 copy-start.1
  128.4 0.0 copy-start.6
  128.4 5.6 %all-to-all-start.1 = ((bf16[64,16,2304]{2,1,0:T(8,128)(2,1)}), bf16[64,16,2304]{2,1,0:T(8,128)(2,1)}, u32[]{:S(2)}, u32[]{:S(2)}) async-start(bf16[64,16,2304]{2,1,0:T(8,128)(2,1)} %bitcast.31), calls=%async_computation.1 | async-start | bytes 9437184 | tf_op jit(solution)/shard_map/all_to_all | solution.py:523
  134.0 0.0 copy-done.4
  134.1 0.0 copy-done
  134.1 0.2 multiply_reduce_fusion
  134.3 0.0 copy-done.3
  134.3 0.8 fusion.2
  135.1 0.0 copy-done.5
  135.1 0.1 copy.35.refs_10_
  135.2 0.0 copy-done.1
  135.2 0.0 copy-start.2
  135.2 0.2 multiply_reduce_fusion.1
  135.4 0.8 fusion.5
  136.2 0.0 copy-done.6
  136.2 0.1 copy.33
  136.3 0.7 broadcast_divide_fusion
  137.0 3.9 %shard_map.133 = (bf16[384,1024]{1,0:T(8,128)(2,1)}, bf16[640,1024]{1,0:T(8,128)(2,1)}, bf16[384,1024]{1,0:T(8,128)(2,1)}, bf16[640,1024]{1,0:T(8,128)(2,1)}, bf...) custom-call(f32[64,2]{1,0:T(8,128)} %get-tuple-element.23.refs_0_, f32[64,2]{1,0:T(8,128)} %get-tuple-element.22.refs_1_, ...), custom_call_target="tpu_custom_call" | custom-call | bytes 1024 | tf_op jit(solution)/shard_map/pallas_call | solution.py:380
  140.9 1.0 pad.4.refs_12_
  141.9 52.1 %all-to-all-done.1 = bf16[64,16,2304]{2,1,0:T(8,128)(2,1)} async-done(((bf16[64,16,2304]{2,1,0:T(8,128)(2,1)}), bf16[64,16,2304]{2,1,0:T(8,128)(2,1)}, u32[]{:S(2)}, u32[]{:S(2)}) %all-to-all-start.1) | async-done | bytes 4718624 | tf_op jit(solution)/shard_map/all_to_all | solution.py:523
  194.1 0.0 copy-done.2
  194.1 8.3 %shard_map.134 = (bf16[64,3584]{1,0:T(8,128)(2,1)}, bf16[64,3584]{1,0:T(8,128)(2,1)}) custom-call(bf16[1024,2304]{1,0:T(8,128)(2,1)} %bitcast.11.far, bf16[384,1024]{1,0:T(8,128)(2,1)} %get-tuple-element.10.refs_0_, bf16[640,1024]{1,0:T(8,128)(2,1)} %get-tuple-element.11.refs_1_, bf16[384,1024]{1,0:T(8,128)(2,1)} %get-tuple-element.12.refs_2_, ...), custom_call_target="tpu_custom_call" | custom-call | bytes 1024 | tf_op jit(solution)/shard_map/pallas_call | solution.py:504
  202.3 3.1 %collective-permute-start = (bf16[1,64,3584]{2,1,0:T(8,128)(2,1)}, bf16[1,64,3584]{2,1,0:T(8,128)(2,1)S(1)}, u32[]{:S(2)}, u32[]{:S(2)}) collective-permute-start(bf16[1,64,3584]{2,1,0:T(8,128)(2,1)} %bitcast.47), channel_id=1, source_target_pairs={{0,64},{64,128},{128,192},{192,0},{1,65},{65,129},{129,193},{193,1... | collective-permute-start | bytes 1376264 | tf_op jit(solution)/shard_map/ppermute | solution.py:528
  205.4 2.2 collective-permute-start.1
  207.6 20.2 %collective-permute-done = bf16[1,64,3584]{2,1,0:T(8,128)(2,1)S(1)} collective-permute-done((bf16[1,64,3584]{2,1,0:T(8,128)(2,1)}, bf16[1,64,3584]{2,1,0:T(8,128)(2,1)S(1)}, u32[]{:S(2)}, u32[]{:S(2)}) %collective-permute-start) | collective-permute-done | bytes 458784 | tf_op jit(solution)/shard_map/ppermute | solution.py:528
  227.8 1.1 collective-permute-done.1
  229.0 0.8 copy.43
  229.7 0.8 copy.44
  (5 shorter events, 0.1 us)
Async XLA Ops:
  128.3 5.7 %copy-start.4 = (f32[1,3584]{1,0:T(1,128)S(1)}, f32[1,3584]{1,0:T(1,128)}, u32[]{:S(2)}) copy-start(f32[1,3584]{1,0:T(1,128)} %refs_11_.1) | copy-start | bytes 43012
  128.3 5.8 %copy-start = (bf16[1,64,3584]{2,1,0:T(8,128)(2,1)S(1)}, bf16[1,64,3584]{2,1,0:T(8,128)(2,1)}, u32[]{:S(2)}) copy-start(bf16[1,64,3584]{2,1,0:T(8,128)(2,1)} %param.14) | copy-start | bytes 1376260
  128.3 6.0 %copy-start.3 = (bf16[1,3584,32]{1,2,0:T(8,128)(2,1)S(1)}, bf16[1,3584,32]{1,2,0:T(8,128)(2,1)}, u32[]{:S(2)}) copy-start(bf16[1,3584,32]{1,2,0:T(8,128)(2,1)} %param.18) | copy-start | bytes 688132
  128.3 6.7 %copy-start.5 = (s32[1,64,2]{1,2,0:T(2,128)S(1)}, s32[1,64,2]{1,2,0:T(2,128)}, u32[]{:S(2)}) copy-start(s32[1,64,2]{1,2,0:T(2,128)} %param.16) | copy-start | bytes 1540
  128.3 6.9 %copy-start.1 = (bf16[1,64,3584]{2,1,0:T(8,128)(2,1)S(1)}, bf16[1,64,3584]{2,1,0:T(8,128)(2,1)}, u32[]{:S(2)}) copy-start(bf16[1,64,3584]{2,1,0:T(8,128)(2,1)} %param.12) | copy-start | bytes 1376260
  128.4 7.8 %copy-start.6 = (s32[1,64,2]{1,2,0:T(2,128)S(1)}, s32[1,64,2]{1,2,0:T(2,128)}, u32[]{:S(2)}) copy-start(s32[1,64,2]{1,2,0:T(2,128)} %param.13) | copy-start | bytes 1540
  128.4 65.7 %all-to-all-start.1 = ((bf16[64,16,2304]{2,1,0:T(8,128)(2,1)}), bf16[64,16,2304]{2,1,0:T(8,128)(2,1)}, u32[]{:S(2)}, u32[]{:S(2)}) async-start(bf16[64,16,2304]{2,1,0:T(8,128)(2,1)} %bitcast.31), calls=%async_computation.1 | async-start | bytes 9437184 | tf_op jit(solution)/shard_map/all_to_all | solution.py:523
  135.2 58.9 %copy-start.2 = (f32[64,2]{1,0:T(8,128)}, f32[64,2]{1,0:T(8,128)S(1)}, u32[]{:S(2)}) copy-start(f32[64,2]{1,0:T(8,128)S(1)} %copy.35.refs_10_) | copy-start | bytes 1540
  202.3 25.5 %collective-permute-start = (bf16[1,64,3584]{2,1,0:T(8,128)(2,1)}, bf16[1,64,3584]{2,1,0:T(8,128)(2,1)S(1)}, u32[]{:S(2)}, u32[]{:S(2)}) collective-permute-start(bf16[1,64,3584]{2,1,0:T(8,128)(2,1)} %bitcast.47), channel_id=1, source_target_pairs={{0,64},{64,128},{128,192},{192,0},{1,65},{65,129},{129,193},{193,1... | collective-permute-start | bytes 1376264 | tf_op jit(solution)/shard_map/ppermute | solution.py:528
  205.4 23.6 %collective-permute-start.1 = (bf16[1,64,3584]{2,1,0:T(8,128)(2,1)}, bf16[1,64,3584]{2,1,0:T(8,128)(2,1)S(1)}, u32[]{:S(2)}, u32[]{:S(2)}) collective-permute-start(bf16[1,64,3584]{2,1,0:T(8,128)(2,1)} %bitcast.46), channel_id=1, source_target_pairs={{0,192},{64,0},{128,64},{192,128},{1,193},{65,1},{129,65},{193,129... | collective-permute-start | bytes 1376264 | tf_op jit(solution)/shard_map/ppermute | solution.py:528

commit v2 on v1

v2 whole, which is shorter than its diff:
```python
import jax
import jax.numpy as jnp
import numpy as np
from jax import lax
from jax.experimental import pallas as pl
from jax.experimental.pallas import tpu as pltpu
from jax.sharding import PartitionSpec as P

epsilon = 1e-06
VMEM_LIMIT = 60 * 1024 * 1024
CAP = 5
LANES = 1152
ROWS = 16
TAIL = 3 * LANES
FAR = pl.BlockSpec(memory_space=pltpu.HBM)
NEAR = pl.BlockSpec(memory_space=pltpu.VMEM)


def selections():
    gather = np.zeros((256, 256), np.float32)
    for i in range(16):
        gather[240 + i, 16 * i + 15] = 1
        for s in range(CAP):
            for g in range(3):
                gather[80 * g + CAP * i + s, 16 * i + 5 * g + s] = 1
    expand = np.zeros((320, 320), np.float32)
    for i in range(64):
        for s in range(CAP):
            expand[CAP * i + s, 64 * s + i] = 1
    whole = expand.reshape(320, CAP, 64).sum(1)
    chunks = np.concatenate([gather, gather.T])
    slots = np.concatenate([expand, expand.T, whole.T])
    return jnp.asarray(chunks, jnp.bfloat16), jnp.asarray(slots, jnp.bfloat16)


def params():
    return dict(
        compiler_params=pltpu.CompilerParams(vmem_limit_bytes=VMEM_LIMIT),
        cost_estimate=pl.CostEstimate(flops=0, bytes_accessed=1024, transcendentals=0),
    )


def f32(x):
    return x.astype(jnp.float32)


def count(hits, axis):
    return jnp.sum(jnp.where(hits, 1.0, 0.0), axis=axis, keepdims=True)


def place_of(position):
    expert = lax.bitwise_and(lax.shift_right_logical(position, 4), 31)
    row = lax.bitwise_and(position, 15)
    block = jnp.where(row >= 5, 1, 0) + jnp.where(row >= 10, 1, 0) + jnp.where(row >= 15, 1, 0)
    return expert, row, block, row - 5 * block


def as_row(column, copies):
    n = column.shape[0]
    shape = (n, copies * n)
    lane = lax.bitwise_and(lax.broadcasted_iota(jnp.int32, shape, 1), n - 1)
    hit = lax.broadcasted_iota(jnp.int32, shape, 0) == lane
    return jnp.sum(jnp.where(hit, column, 0.0), axis=0, keepdims=True)


def pack(units, gain, routes):
    n, m = len(units), len(routes)
    tokens, width = units[0][0].shape
    half_rows = 32 * ROWS
    operands = [*routes, gain, *[rows for rows, _, _ in units]]

    def kernel(*refs):
        far, out = refs[: n + m + 1], refs[n + m + 1]
        near = refs[n + m + 2 : 2 * (n + m) + 3]
        made, low, high, sems = refs[2 * (n + m) + 3 :]
        loads = [
            pltpu.make_async_copy(src, dst, sems.at[i]) for i, (src, dst) in enumerate(zip(far, near))
        ]
        for load in loads:
            load.start()
        for load in loads[: m + 1]:
            load.wait()
        gain_ref = near[m]
        shape = (half_rows, 2 * tokens)
        expert, row, block, slot = place_of(lax.broadcasted_iota(jnp.int32, shape, 0))
        right = lax.broadcasted_iota(jnp.int32, shape, 1) >= tokens
        stores = []
        for route in range(m):
            ids = f32(near[route][...])
            first, second = ids[:, 0:1], ids[:, 1:2]
            first_r, second_r = as_row(first, 2), as_row(second, 2)
            square = (tokens, 2 * tokens)
            lane = lax.bitwise_and(lax.broadcasted_iota(jnp.int32, square, 1), tokens - 1)
            before = lax.broadcasted_iota(jnp.int32, square, 0) < lane
            slot_0 = count((first == first_r) & before, 0)
            slot_1 = count(first == second_r, 0) + count((second == second_r) & before, 0)
            key_0, key_1 = first_r * 8 + slot_0, second_r * 8 + slot_1

            def hits(key, key_0=key_0, key_1=key_1):
                key = f32(key)
                return (key_0 == key) | (key_1 == key)

            def matrix(mask):
                return jnp.where(mask, 1.0, 0.0).astype(jnp.bfloat16)

            own = hits(expert * 8 + slot)
            pick_low = matrix(own & (block == jnp.where(right, 1, 0)))
            third = own & (block == 2) & ~right
            pick_rest = matrix(third)
            picks = [
                matrix(third | (hits(expert * 8 + s) & (row == 15) & right)) for s in range(CAP)
            ]
            for u in range(n):
                if units[u][2] != route:
                    continue
                loads[m + 1 + u].wait()
                x = near[m + 1 + u][...]
                if units[u][1]:
                    v = f32(x)
                    inverse = lax.rsqrt(jnp.mean(v * v, axis=-1, keepdims=True) + epsilon)
                    x = (v * inverse * gain_ref[...]).astype(jnp.bfloat16)
                low[0:tokens, :] = x[:, :LANES]
                low[tokens:, :] = x[:, LANES : 2 * LANES]
                high[0:tokens, :] = x[:, 2 * LANES : TAIL]
                high[tokens:, :] = jnp.zeros((tokens, LANES), jnp.bfloat16)
                for s in range(CAP):
                    high[tokens:, 128 * s : 128 * s + 128] = x[:, TAIL:]
                for s in range(9):
                    cols = slice(128 * s, 128 * s + 128)
                    part = jnp.dot(pick_low, low[:, cols], preferred_element_type=jnp.float32)
                    part += jnp.dot(
                        picks[s] if s < CAP else pick_rest,
                        high[:, cols],
                        preferred_element_type=jnp.float32,
                    )
                    made[:, u * LANES + 128 * s : u * LANES + 128 * s + 128] = part.astype(
                        jnp.bfloat16
                    )
                lanes = pl.ds(u * LANES, LANES)
                for r in range(2):
                    stores.append(
                        pltpu.make_async_copy(
                            made.at[:, lanes],
                            out.at[pl.ds(half_rows * r, half_rows), lanes],
                            sems.at[n + m + 1 + 2 * u + r],
                        )
                    )
                    stores[-1].start()
        for store in stores:
            store.wait()

    return pl.pallas_call(
        kernel,
        out_shape=jax.ShapeDtypeStruct((2 * half_rows, n * LANES), jnp.bfloat16),
        in_specs=[FAR] * (n + m + 1),
        out_specs=FAR,
        scratch_shapes=[pltpu.VMEM(v.shape, v.dtype) for v in operands]
        + [
            pltpu.VMEM((half_rows, n * LANES), jnp.bfloat16),
            pltpu.VMEM((2 * tokens, LANES), jnp.bfloat16),
            pltpu.VMEM((2 * tokens, LANES), jnp.bfloat16),
            pltpu.SemaphoreType.DMA((3 * n + m + 1,)),
        ],
        **params(),
    )(*operands)


def unpack(chunks, offset, tables, x, start, last, stacked):
    gather, expand = tables

    for b in range(4):
        held = slice(256 * b, 256 * b + 256)
        rows = slice(start + 80 * b, start + 80 * b + 80)
        for c in range(3):
            part = jnp.dot(
                gather[:256, :],
                chunks[held, offset + 384 * c : offset + 384 * c + 384],
                preferred_element_type=jnp.float32,
            ).astype(jnp.bfloat16)
            for g in range(3):
                at = g * LANES + 384 * c
                x[rows, at : at + 384] = part[80 * g : 80 * g + 80]
            last[16 * b : 16 * b + 16, 384 * c : 384 * c + 384] = part[240:]
    for s in range(CAP):
        stacked[64 * s : 64 * s + 64, :] = last[:, 128 * s : 128 * s + 128]
    x[start : start + 320, TAIL:] = jnp.dot(
        expand[:320, :], stacked[...], preferred_element_type=jnp.float32
    ).astype(jnp.bfloat16)


def repack(chunks, offset, tables, made, rest, extra=None):
    gather, expand = tables
    tail = jnp.dot(
        expand[320:640, :], rest[...], preferred_element_type=jnp.float32
    ).astype(jnp.bfloat16)
    spare = jnp.zeros((64, 128), jnp.bfloat16)
    if extra is not None:
        spare = jnp.dot(
            expand[640:, :], extra[...], preferred_element_type=jnp.float32
        ).astype(jnp.bfloat16)
    for b in range(4):
        at = slice(256 * b + 240, 256 * b + 256)
        for s in range(CAP):
            made[at, 128 * s : 128 * s + 128] = tail[64 * s + 16 * b : 64 * s + 16 * b + 16]
        made[at, 640:768] = spare[16 * b : 16 * b + 16]
        made[at, 768:] = jnp.zeros((16, LANES - 768), jnp.bfloat16)

    for b in range(4):
        held = slice(256 * b, 256 * b + 256)
        chunks[held, offset : offset + LANES] = jnp.dot(
            gather[256:, :], made[held, :], preferred_element_type=jnp.float32
        ).astype(jnp.bfloat16)


def put_result(made, rest, product):
    for g in range(3):
        part = product(pl.ds(g * LANES, LANES)).astype(jnp.bfloat16)
        for b in range(4):
            made[256 * b + 80 * g : 256 * b + 80 * g + 80, :] = part[80 * b : 80 * b + 80]
    rest[...] = product(pl.ds(TAIL, 128)).astype(jnp.bfloat16)


def load_all(far, near, sems, first=0):
    return [
        pltpu.make_async_copy(src, dst, sems.at[first + n])
        for n, (src, dst) in enumerate(zip(far, near))
    ]


def experts_forward(chunks, offset, tables, weights):
    width, units = weights[0].shape
    half = units // 2

    def kernel(far, *refs):
        far_in, far_out = refs[:5], refs[5]
        near, gather, expand, wg, wu, wd, x, hidden, made, rest, last, stacked, sems = refs[6:]
        tables = (gather, expand)
        part = pltpu.make_async_copy(far.at[:, pl.ds(offset, LANES)], near, sems.at[0])
        loads = load_all(
            (far_in[0], far_in[1], far_in[4]), (gather, expand, wd), sems, 1
        )
        pieces = []
        for k in range(2):
            cols = pl.ds(half * k, half)
            pieces += load_all(
                (far_in[2].at[:, cols], far_in[3].at[:, cols]),
                (wg.at[:, cols], wu.at[:, cols]),
                sems,
                4 + 2 * k,
            )
        for load in (part, loads[0], loads[1], *pieces, loads[2]):
            load.start()
        part.wait()
        loads[0].wait()
        loads[1].wait()
        unpack(near, 0, tables, x, 0, last, stacked)
        for k in range(2):
            pieces[2 * k].wait()
            pieces[2 * k + 1].wait()
            cols = pl.ds(half * k, half)
            gate = jnp.dot(x[...], wg[:, cols], preferred_element_type=jnp.float32)
            upper = jnp.dot(x[...], wu[:, cols], preferred_element_type=jnp.float32)
            hidden[:, cols] = (gate * jax.nn.sigmoid(gate) * upper).astype(jnp.bfloat16)
        loads[2].wait()
        put_result(
            made,
            rest,
            lambda cols: jnp.dot(hidden[...], wd[:, cols], preferred_element_type=jnp.float32),
        )
        repack(near, 0, tables, made, rest)
        store = pltpu.make_async_copy(near, far_out, sems.at[8])
        store.start()
        store.wait()

    rows = chunks.shape[0]
    return pl.pallas_call(
        kernel,
        out_shape=jax.ShapeDtypeStruct((rows, LANES), jnp.bfloat16),
        in_specs=[FAR] * 6,
        out_specs=FAR,
        scratch_shapes=[pltpu.VMEM((rows, LANES), jnp.bfloat16)]
        + [pltpu.VMEM(v.shape, v.dtype) for v in (*tables, *weights)]
        + [
            pltpu.VMEM((320, width), jnp.bfloat16),
            pltpu.VMEM((320, units), jnp.bfloat16),
            pltpu.VMEM((1024, LANES), jnp.bfloat16),
            pltpu.VMEM((320, 128), jnp.bfloat16),
            pltpu.VMEM((64, LANES), jnp.bfloat16),
            pltpu.VMEM((320, 128), jnp.bfloat16),
            pltpu.SemaphoreType.DMA((9,)),
        ],
        **params(),
    )(chunks, *tables, *weights)


def experts_backward(chunks, tables, weights, after):
    width, units = weights[0].shape
    contract = (((1,), (1,)), ((), ()))

    def kernel(far, *refs):
        far_in, far_out = refs[:5], refs[6]
        near, gather, expand, wg, wu, wd = refs[7:13]
        x, cot, d_gate, d_up, made, rest, extra, last, stacked, sems = refs[13:]
        tables = (gather, expand)
        parts = load_all(
            [far.at[:, pl.ds(u * LANES, LANES)] for u in range(2)],
            [near.at[:, pl.ds(u * LANES, LANES)] for u in range(2)],
            sems,
        )
        loads = load_all(far_in, (gather, expand, wg, wu, wd), sems, 2)
        for load in (parts[0], loads[0], loads[1], parts[1], *loads[2:]):
            load.start()
        parts[0].wait()
        loads[0].wait()
        loads[1].wait()
        unpack(near, 0, tables, x, 0, last, stacked)
        parts[1].wait()
        unpack(near, LANES, tables, cot, 0, last, stacked)
        for load in loads[2:]:
            load.wait()

        def step(k, inner):
            cols = pl.ds(pl.multiple_of(k * 256, 256), 256)
            gate = jnp.dot(x[...], wg[:, cols], preferred_element_type=jnp.float32)
            upper = jnp.dot(x[...], wu[:, cols], preferred_element_type=jnp.float32)
            d_hidden = lax.dot_general(
                cot[...], wd[cols, :], contract, preferred_element_type=jnp.float32
            )
            s = jax.nn.sigmoid(gate)
            active = gate * s
            value = f32((active * upper).astype(jnp.bfloat16))
            d_gate[:, cols] = (d_hidden * upper * s * (1.0 + gate * (1.0 - s))).astype(
                jnp.bfloat16
            )
            d_up[:, cols] = (d_hidden * active).astype(jnp.bfloat16)
            return inner + jnp.sum(value * d_hidden, axis=1, keepdims=True)

        inner = lax.fori_loop(0, units // 256, step, jnp.zeros((320, 1), jnp.float32))
        slot = lax.rem(lax.broadcasted_iota(jnp.int32, (320, 128), 0), CAP)
        lane = lax.broadcasted_iota(jnp.int32, (320, 128), 1)
        extra[...] = jnp.where(slot == lane, inner, 0.0).astype(jnp.bfloat16)

        def back(cols):
            return lax.dot_general(
                d_gate[...], wg[cols, :], contract, preferred_element_type=jnp.float32
            ) + lax.dot_general(
                d_up[...], wu[cols, :], contract, preferred_element_type=jnp.float32
            )

        put_result(made, rest, back)
        repack(near, 0, tables, made, rest, extra)
        store = pltpu.make_async_copy(near.at[:, pl.ds(0, LANES)], far_out, sems.at[7])
        store.start()
        store.wait()

    rows = chunks.shape[0]
    return pl.pallas_call(
        kernel,
        out_shape=jax.ShapeDtypeStruct((rows, LANES), jnp.bfloat16),
        in_specs=[FAR] * 6 + [pl.BlockSpec(memory_space=pl.ANY)],
        out_specs=FAR,
        scratch_shapes=[pltpu.VMEM((rows, 2 * LANES), jnp.bfloat16)]
        + [pltpu.VMEM(v.shape, v.dtype) for v in (*tables, *weights)]
        + [
            pltpu.VMEM((320, width), jnp.bfloat16),
            pltpu.VMEM((320, width), jnp.bfloat16),
            pltpu.VMEM((320, units), jnp.bfloat16),
            pltpu.VMEM((320, units), jnp.bfloat16),
            pltpu.VMEM((1024, LANES), jnp.bfloat16),
            pltpu.VMEM((320, 128), jnp.bfloat16),
            pltpu.VMEM((320, 128), jnp.bfloat16),
            pltpu.VMEM((64, LANES), jnp.bfloat16),
            pltpu.VMEM((320, 128), jnp.bfloat16),
            pltpu.SemaphoreType.DMA((8,)),
        ],
        **params(),
    )(chunks, *tables, *weights, after)


def spread_weights(weights, routes):
    tokens = routes[0].shape[0]
    total_rows = 64 * ROWS
    n = len(routes)

    def kernel(*refs):
        w_refs, id_refs, outs = refs[:n], refs[n : 2 * n], refs[2 * n :]
        square = (tokens, tokens)
        before = lax.broadcasted_iota(jnp.int32, square, 1) < lax.broadcasted_iota(
            jnp.int32, square, 0
        )
        shape = (tokens, total_rows)
        expert, row, block, slot = place_of(lax.broadcasted_iota(jnp.int32, shape, 1))
        place = lax.broadcasted_iota(jnp.int32, (tokens, 64 * CAP), 1)
        place = lax.bitwise_and(place, 31) * 8 + lax.shift_right_logical(place, 6)
        for at in range(n):
            w, ids = w_refs[at], f32(id_refs[at][...])
            first, second = ids[:, 0:1], ids[:, 1:2]
            first_r, second_r = as_row(first, 1), as_row(second, 1)
            slot_0 = count((first == first_r) & before, 1)
            slot_1 = count(second == first_r, 1) + count((second == second_r) & before, 1)
            key_0, key_1 = first * 8 + slot_0, second * 8 + slot_1

            def spread(key, w=w, key_0=key_0, key_1=key_1):
                key = f32(key)
                total = jnp.where(key_0 == key, w[:, 0:1], 0.0) + jnp.where(
                    key_1 == key, w[:, 1:2], 0.0
                )
                upper = f32(total.astype(jnp.bfloat16))
                return upper, total - upper

            for i, value in enumerate(spread(expert * 8 + slot)):
                for g in range(3):
                    start = 2 * tokens * g + tokens * i
                    outs[2 * at][start : start + tokens, :] = jnp.where(
                        block == g, value, 0.0
                    ).astype(jnp.bfloat16)
            for i, value in enumerate(spread(place)):
                outs[2 * at + 1][tokens * i : tokens * i + tokens, :] = value.astype(jnp.bfloat16)
            if at == n - 1:
                source = lax.broadcasted_iota(jnp.int32, (tokens, 64), 1)
                source = f32(lax.bitwise_and(source, 31))
                for k, (chosen, number) in enumerate(((first, slot_0), (second, slot_1))):
                    outs[2 * n][tokens * k : tokens * k + tokens, :] = jnp.where(
                        source == chosen, 1.0, 0.0
                    ).astype(jnp.bfloat16)
                    outs[2 * n + 1][:, 128 * k : 128 * k + 128] = jnp.broadcast_to(
                        number, (tokens, 128)
                    )

    shapes = [(6 * tokens, total_rows), (2 * tokens, 64 * CAP)] * n + [(2 * tokens, 64)]
    return pl.pallas_call(
        kernel,
        out_shape=[jax.ShapeDtypeStruct(shape, jnp.bfloat16) for shape in shapes]
        + [jax.ShapeDtypeStruct((tokens, 256), jnp.float32)],
        in_specs=[NEAR] * (2 * n),
        out_specs=[NEAR] * (2 * n + 2),
        **params(),
    )(*weights, *routes)


def last_rows(near, columns):
    shape = (64, 64 * ROWS)
    wanted = lax.broadcasted_iota(jnp.int32, shape, 0) * ROWS + (ROWS - 1)
    pick = jnp.where(wanted == lax.broadcasted_iota(jnp.int32, shape, 1), 1.0, 0.0)
    return jnp.dot(
        pick.astype(jnp.bfloat16), near[:, :columns], preferred_element_type=jnp.float32
    ).astype(jnp.bfloat16)


def add_up(near, rows_15, stacked, parts, tails, store):
    tokens = tails.shape[0] // 2
    for s in range(CAP):
        stacked[64 * s : 64 * s + 64, :] = rows_15[:, 128 * s : 128 * s + 128]
    rest = jnp.dot(tails[...], stacked[...], preferred_element_type=jnp.float32)
    store(TAIL, 128, rest[:tokens] + rest[tokens:])
    for c in range(3):
        part = jnp.dot(
            parts[...], near[:, 384 * c : 384 * c + 384], preferred_element_type=jnp.float32
        )
        for g in range(3):
            at = 2 * tokens * g
            store(
                g * LANES + 384 * c,
                384,
                part[at : at + tokens] + part[at + tokens : at + 2 * tokens],
            )


def finish_forward(chunks, parts, tails, rows):
    tokens, width = rows.shape
    operands = [chunks, parts, tails, rows]

    def kernel(*refs):
        out, held, result, stacked, sems = refs[4], refs[5:9], refs[9], refs[10], refs[11]
        near, parts, tails, v = held
        loads = load_all(refs[:4], held, sems)
        for load in loads:
            load.start()
        for load in loads:
            load.wait()

        def put(at, size, value):
            result[:, at : at + size] = (f32(v[:, at : at + size]) + value).astype(jnp.bfloat16)

        add_up(near, last_rows(near, 640), stacked, parts, tails, put)
        store = pltpu.make_async_copy(result, out, sems.at[4])
        store.start()
        store.wait()

    return pl.pallas_call(
        kernel,
        out_shape=jax.ShapeDtypeStruct((tokens, width), jnp.bfloat16),
        in_specs=[FAR] * 4,
        out_specs=FAR,
        scratch_shapes=[pltpu.VMEM(v.shape, v.dtype) for v in operands]
        + [
            pltpu.VMEM((tokens, width), jnp.bfloat16),
            pltpu.VMEM((64 * CAP, 128), jnp.bfloat16),
            pltpu.SemaphoreType.DMA((5,)),
        ],
        **params(),
    )(*operands)


def finish_backward(chunks, spreads, rows, cotangent, routes, picked, gain, router_rows):
    tokens, width = rows.shape
    operands = [chunks, *spreads, rows, cotangent, routes, picked, gain, router_rows]
    n = len(operands)

    def kernel(*refs):
        out, held = refs[n], refs[n + 1 : 2 * n + 1]
        gradient, total, stacked, sems = refs[2 * n + 1 :]
        near, parts, tails, picks, slots, v_ref, cot, ids, chosen, gain_ref, router_ref = held
        loads = load_all(refs[:n], held, sems)
        for load in loads:
            load.start()
        for load in loads:
            load.wait()
        rows_15 = last_rows(near, 768)
        found = jnp.dot(picks[...], rows_15[:, 640:], preferred_element_type=jnp.float32)
        lane = f32(lax.broadcasted_iota(jnp.int32, (tokens, 128), 1))
        inner = [
            jnp.sum(
                jnp.where(
                    lane == slots[:, 128 * k : 128 * k + 128],
                    found[tokens * k : tokens * k + tokens],
                    0.0,
                ),
                axis=1,
                keepdims=True,
            )
            for k in range(2)
        ]
        scores = [chosen[:, k : k + 1] for k in range(2)]
        whole = scores[0] + scores[1]
        mean = (inner[0] * scores[0] + inner[1] * scores[1]) / whole
        numbers = f32(ids[...])
        d_logits = jnp.zeros((tokens, 128), jnp.float32)
        for k in range(2):
            d_logit = (inner[k] - mean) / whole * scores[k] * (1.0 - scores[k])
            d_logits += jnp.where(lane == numbers[:, k : k + 1], d_logit, 0.0)
        pieces, left = [], d_logits
        for _ in range(3):
            pieces.append(left.astype(jnp.bfloat16))
            left = left - f32(pieces[-1])
        pieces = jnp.concatenate(pieces, axis=0)

        def keep(at, size, value):
            routed = jnp.dot(
                pieces, router_ref[:, at : at + size], preferred_element_type=jnp.float32
            )
            for i in range(3):
                value += routed[tokens * i : tokens * i + tokens]
            total[:, at : at + size] = value * gain_ref[:, at : at + size]

        add_up(near, rows_15, stacked, parts, tails, keep)
        v = f32(v_ref[...])
        inverse = lax.rsqrt(jnp.mean(v * v, axis=-1, keepdims=True) + epsilon)
        projected = jnp.mean(v * total[...], axis=-1, keepdims=True)
        d_rows = total[...] * inverse - v * (inverse * inverse * inverse * projected)
        gradient[...] = (f32(cot[...]) + d_rows).astype(jnp.bfloat16)
        store = pltpu.make_async_copy(gradient, out, sems.at[n])
        store.start()
        store.wait()

    return pl.pallas_call(
        kernel,
        out_shape=jax.ShapeDtypeStruct((tokens, width), jnp.bfloat16),
        in_specs=[FAR] * n,
        out_specs=FAR,
        scratch_shapes=[pltpu.VMEM(v.shape, v.dtype) for v in operands]
        + [
            pltpu.VMEM((tokens, width), jnp.bfloat16),
            pltpu.VMEM((tokens, width), jnp.float32),
            pltpu.VMEM((64 * CAP, 128), jnp.bfloat16),
            pltpu.SemaphoreType.DMA((n + 1,)),
        ],
        **params(),
    )(*operands)


def swapped(chunks):
    shape = chunks.shape
    chunks = chunks.reshape(shape[0] // ROWS, ROWS, shape[1])
    return lax.all_to_all(chunks, "expert", 0, 0, tiled=True).reshape(shape)


def passed_along(x, axis, by):
    n = lax.axis_size(axis)
    return lax.ppermute(x, axis, [(i, (i + by) % n) for i in range(n)])


def normalise(values, gain_row):
    inverse = lax.rsqrt(jnp.mean(values * values, axis=-1, keepdims=True) + epsilon)
    return values * inverse * gain_row


def picked_scores(values, gain_row, router_map, routes):
    normed = normalise(values.astype(jnp.float32), gain_row)
    logits = jnp.dot(normed, router_map.astype(jnp.float32), precision=lax.Precision.HIGHEST)
    scores = jax.nn.sigmoid(logits)
    choices_axis = jnp.arange(router_map.shape[1], dtype=jnp.int32)
    onehot = (routes[:, :, None] == choices_axis[None, None, :]).astype(scores.dtype)
    return jnp.sum(onehot * scores[:, None, :], axis=-1)


def body(
    forward_rows,
    forward_routes,
    saved_rows,
    cotangent,
    backward_routes,
    norm_gain,
    router,
    gate_weight,
    up_weight,
    down_weight,
):
    gain_row, router_map = norm_gain[0], router[0]
    weights = (gate_weight[0, 0], up_weight[0, 0], down_weight[0, 0])
    tables = selections()
    backward_ids, forward_ids = backward_routes[0], forward_routes[0]

    saved, cotan, forward = saved_rows[0], cotangent[0], forward_rows[0]

    sent = pack(
        [(saved, True, 0), (cotan, False, 0), (forward, True, 1)],
        norm_gain,
        [backward_ids, forward_ids],
    )
    received = swapped(sent)
    backward_scores = picked_scores(saved, gain_row, router_map, backward_ids)
    forward_scores = picked_scores(forward, gain_row, router_map, forward_ids)
    spreads = spread_weights(
        [v / jnp.sum(v, axis=1, keepdims=True) for v in (forward_scores, backward_scores)],
        [forward_ids, backward_ids],
    )
    forward_chunks = experts_forward(received, 2 * LANES, tables, weights)
    backward_chunks = experts_backward(received, tables, weights, forward_chunks)
    forward_back, backward_back = swapped(forward_chunks), swapped(backward_chunks)
    router_rows = jnp.pad(router_map.T, ((0, 128 - router_map.shape[1]), (0, 0)))
    result = finish_forward(forward_back, spreads[0], spreads[1], forward)
    gradient = finish_backward(
        backward_back,
        spreads[2:],
        saved,
        cotan,
        backward_ids,
        backward_scores,
        norm_gain,
        router_rows,
    )
    backward_next = passed_along(gradient[None], "pipe", -1)
    forward_next = passed_along(result[None], "pipe", 1)
    return (forward_next, backward_next)


def solution(mesh):
    in_specs = (
        P("pipe", "expert", None),
        P("pipe", "expert", None),
        P("pipe", "expert", None),
        P("pipe", "expert", None),
        P("pipe", "expert", None),
        P("pipe", None),
        P("pipe", None, None),
        P("pipe", "expert", None, None),
        P("pipe", "expert", None, None),
        P("pipe", "expert", None, None),
    )
    out_specs = (P("pipe", "expert", None), P("pipe", "expert", None))
    return jax.shard_map(body, mesh=mesh, in_specs=in_specs, out_specs=out_specs, check_vma=False)
```

time: 231 us -> 225 us (0.974)
  waiting for transfers between devices: 73.5 us -> 54.9 us
  starting transfers between devices: 10.9 us -> 18.2 us
  local copies, waits for them, and re-layouts: 5.53 us -> 8.33 us
    all_to_all x1 -> x2, waiting for transfers between devices: 52.1 us -> 36.3 us  [swapped(): return lax.all_to_all(chunks, 'expert', 0, 0, tiled=True).reshape(shape)]
    all_to_all x1 -> x2, starting transfers between devices: 5.63 us -> 9.66 us  [swapped(): return lax.all_to_all(chunks, 'expert', 0, 0, tiled=True).reshape(shape)]
    ppermute x2, starting transfers between devices: 5.29 us -> 8.5 us  [passed_along(): return lax.ppermute(x, axis, [(i, (i + by) % n) for i in range(n)])]
    unnamed x16 -> x18, local copies, waits for them, and re-layouts: 1.58 us -> 4.39 us
    ppermute x2, waiting for transfers between devices: 21.3 us -> 18.5 us  [passed_along(): return lax.ppermute(x, axis, [(i, (i + by) % n) for i in range(n)])]
    pallas_call x2 -> x4, Pallas kernels: 33.9 us -> 35.9 us  [the longest x1 15.4 us: experts_backward(): pl.pallas_call(kernel, out_shape=jax.ShapeDtypeStruct((rows, LANES), jnp....]
  transfers between devices with their start and end apart: 3 -> 4, of which waited for: 3 -> 4; matrix products, arithmetic and copies ran while one was open for 2% -> 2% of each run, Pallas kernels for 2% -> 13%
where the time goes in v2:
time: 225 us; the launch traced here: 223 us
  blocking collectives  93 us (41%)
  waiting for transfers between devices  54.9 us (24%)
  Pallas kernels  44.7 us (20%)
  starting transfers between devices  18.2 us (8%)
  local copies, waits for them, and re-layouts  8.33 us (4%)
    all_to_all x1, blocking collectives, swapped(): return lax.all_to_all(chunks, 'expert', 0, 0, tiled=True).reshape(shape)  93 us
    all_to_all x2, waiting for transfers between devices, swapped(): return lax.all_to_all(chunks, 'expert', 0, 0, tiled=True).reshape(shape)  36.3 us
    ppermute x2, waiting for transfers between devices, passed_along(): return lax.ppermute(x, axis, [(i, (i + by) % n) for i in range(n)])  18.5 us
    pallas_call x1, Pallas kernels, experts_backward(): pl.pallas_call(kernel, out_shape=jax.ShapeDtypeStruct((rows, LANES), jnp....  15.4 us
    pallas_call x1, Pallas kernels, experts_forward(): pl.pallas_call(kernel, out_shape=jax.ShapeDtypeStruct((rows, LANES), jnp....  9.76 us
    all_to_all x2, starting transfers between devices, swapped(): return lax.all_to_all(chunks, 'expert', 0, 0, tiled=True).reshape(shape)  9.66 us
    ppermute x2, starting transfers between devices, passed_along(): return lax.ppermute(x, axis, [(i, (i + by) % n) for i in range(n)])  8.5 us
    pallas_call x1, Pallas kernels, finish_backward(): pl.pallas_call(kernel, out_shape=jax.ShapeDtypeStruct((tokens, width), jn...  6.21 us
  transfers between devices with their start and end apart: 4, of which 4 were waited for; matrix products, arithmetic and copies ran while one was open for 2% of the time, Pallas kernels for 13%

profile of v2, /device:TPU:1, one launch (start us, length us, event | category | flops | bytes accessed | tf_op | source)
XLA Modules:
  0.0 223.3 jit_solution(11092548480812504043)
XLA Ops:
  0.6 1.4 copy.31.refs_0_.refs_3_.refs_7_
  2.0 1.4 copy.32.refs_1_.refs_2_
  3.4 6.2 %shard_map.131 = bf16[1024,3456]{1,0:T(8,128)(2,1)} custom-call(s32[64,2]{1,0:T(8,128)} %copy.31.refs_0_.refs_3_.refs_7_, s32[64,2]{1,0:T(8,128)} %copy.32.refs_1_.refs_2_, f32[1,3584]{1,0:T(1,128)} %refs_9_.1, bf16[64,3584]{1,0:T(8,128)(2,1)} %bitcast.44, bf16[64,3584]{1,0:T(8,128)(2,1)} %bitcast.48, bf16[64,3584]{1,0:T(8,128)(2,1)} %bitcast.46), custom_call_target="tpu_custom_call" | custom-call | bytes 1024 | tf_op jit(solution)/shard_map/pallas_call | solution.py:152
  9.6 93.0 %all_to_all.15 = bf16[64,16,3456]{2,1,0:T(8,128)(2,1)} all-to-all(bf16[64,16,3456]{2,1,0:T(8,128)(2,1)} %bitcast.33), channel_id=1, replica_groups=mesh['pipe'=4,'expert'=64] {'expert'}, dimensions={0} | all-to-all | bytes 14155776 | tf_op jit(solution)/shard_map/all_to_all | solution.py:585
  102.6 9.8 %shard_map.132.refs_5_ = bf16[1024,1152]{1,0:T(8,128)(2,1)} custom-call(bf16[1024,3456]{1,0:T(8,128)(2,1)} %bitcast.31, bf16[512,256]{1,0:T(8,128)(2,1)} %constant.19.clone.refs_0_, bf16[704,320]{1,0:T(8,128)(2,1)} %constant.20.clone.refs_1_, bf16[3584,512]{1,0:T(8,128)(2,1)} %bitcast.35, bf16[3584,512]{1,0:T(8,128)(2,1)} %bitcast.37, bf16[512,3584]{1,0:T(8,128)(2,1)} %bitcast.39), custom_call_target="tpu_custom_call" | custom-call | bytes 1024 | tf_op jit(solution)/shard_map/pallas_call | solution.py:276
  112.4 4.7 %all-to-all-start.1 = ((bf16[64,16,1152]{2,1,0:T(8,128)(2,1)}), bf16[64,16,1152]{2,1,0:T(8,128)(2,1)S(1)}, u32[]{:S(2)}, u32[]{:S(2)}) async-start(bf16[64,16,1152]{2,1,0:T(8,128)(2,1)} %bitcast.34), calls=%async_computation.1 | async-start | bytes 4718592 | tf_op jit(solution)/shard_map/all_to_all | solution.py:585
  117.1 15.4 %shard_map.135 = bf16[1024,1152]{1,0:T(8,128)(2,1)} custom-call(bf16[1024,3456]{1,0:T(8,128)(2,1)} %bitcast.32, bf16[512,256]{1,0:T(8,128)(2,1)} %constant.19.clone.refs_0_, bf16[704,320]{1,0:T(8,128)(2,1)} %constant.20.clone.refs_1_, bf16[3584,512]{1,0:T(8,128)(2,1)} %bitcast.36, bf16[3584,512]{1,0:T(8,128)(2,1)} %bitcast.38, bf16[512,3584]{1,0:T(8,128)(2,1)} %bitcast.40, ...), custom_call_target="tpu_custom_call" | custom-call | bytes 1024 | tf_op jit(solution)/shard_map/pallas_call | solution.py:357
  132.5 0.0 copy-start.6
  132.5 0.0 copy-start.2
  132.5 0.0 copy-start.5
  132.6 0.0 copy-start.7
  132.6 0.0 copy-start.3
  132.6 16.3 %all-to-all-done.1 = bf16[64,16,1152]{2,1,0:T(8,128)(2,1)S(1)} async-done(((bf16[64,16,1152]{2,1,0:T(8,128)(2,1)}), bf16[64,16,1152]{2,1,0:T(8,128)(2,1)S(1)}, u32[]{:S(2)}, u32[]{:S(2)}) %all-to-all-start.1) | async-done | bytes 2359328 | tf_op jit(solution)/shard_map/all_to_all | solution.py:585
  148.9 0.0 copy-start.1
  148.9 1.4 copy-done.1
  150.3 5.0 %all-to-all-start.2 = ((bf16[64,16,1152]{2,1,0:T(8,128)(2,1)}), bf16[64,16,1152]{2,1,0:T(8,128)(2,1)S(1)}, u32[]{:S(2)}, u32[]{:S(2)}) async-start(bf16[64,16,1152]{2,1,0:T(8,128)(2,1)} %bitcast.41), calls=%async_computation.2 | async-start | bytes 4718592 | tf_op jit(solution)/shard_map/all_to_all | solution.py:585
  155.3 0.0 copy-done.6
  155.3 0.0 copy-done.2
  155.3 0.2 multiply_reduce_fusion
  155.5 0.0 copy-done.5
  155.5 0.8 fusion.2
  156.3 0.0 copy-done.7
  156.4 0.1 copy.35.refs_8_
  156.5 0.0 copy-done.3
  156.5 0.0 copy-start.4
  156.5 0.2 multiply_reduce_fusion.1
  156.7 0.8 fusion.5
  157.5 0.7 select_reduce_fusion.2
  158.2 0.1 copy.33
  158.3 0.7 broadcast_divide_fusion
  159.0 2.5 %shard_map.133 = (bf16[384,1024]{1,0:T(8,128)(2,1)}, bf16[128,320]{1,0:T(8,128)(2,1)}, bf16[384,1024]{1,0:T(8,128)(2,1)}, bf16[128,320]{1,0:T(8,128)(2,1)}, bf16[128,64]{1,0:T(8,128)(2,1)}, /*index=5*/f32[64,256]{1,0:T(8,128)}) custom-call(f32[64,2]{1,0:T(8,128)} %get-tuple-element.19.refs_0_, f32[64,2]{1,0:T(8,128)} %get-tuple-element.18.refs_1_, ...), custom_call_target="tpu_custom_call" | custom-call | bytes 1024 | tf_op jit(solution)/shard_map/pallas_call | solution.py:431
  161.5 1.0 pad.4.refs_10_
  162.5 4.6 %shard_map.134 = bf16[64,3584]{1,0:T(8,128)(2,1)} custom-call(bf16[1024,1152]{1,0:T(8,128)(2,1)} %bitcast.43, bf16[384,1024]{1,0:T(8,128)(2,1)} %get-tuple-element.8.refs_1_, bf16[128,320]{1,0:T(8,128)(2,1)} %get-tuple-element.9.refs_2_, bf16[64,3584]{1,0:T(8,128)(2,1)} %bitcast.47), custom_call_target="tpu_custom_call" | custom-call | bytes 1024 | tf_op jit(solution)/shard_map/pallas_call | solution.py:490
  167.1 3.3 %collective-permute-start = (bf16[1,64,3584]{2,1,0:T(8,128)(2,1)}, bf16[1,64,3584]{2,1,0:T(8,128)(2,1)S(1)}, u32[]{:S(2)}, u32[]{:S(2)}) collective-permute-start(bf16[1,64,3584]{2,1,0:T(8,128)(2,1)} %bitcast.51), channel_id=1, source_target_pairs={{0,64},{64,128},{128,192},{192,0},{1,65},{65,129},{129,193},{193,1... | collective-permute-start | bytes 1376264 | tf_op jit(solution)/shard_map/ppermute | solution.py:590
  170.4 20.0 %all-to-all-done.2 = bf16[64,16,1152]{2,1,0:T(8,128)(2,1)S(1)} async-done(((bf16[64,16,1152]{2,1,0:T(8,128)(2,1)}), bf16[64,16,1152]{2,1,0:T(8,128)(2,1)S(1)}, u32[]{:S(2)}, u32[]{:S(2)}) %all-to-all-start.2) | async-done | bytes 2359328 | tf_op jit(solution)/shard_map/all_to_all | solution.py:585
  190.4 0.0 copy-start
  190.4 0.0 copy-done.4
  190.4 1.4 copy-done
  191.8 6.2 %shard_map.136 = bf16[64,3584]{1,0:T(8,128)(2,1)} custom-call(bf16[1024,1152]{1,0:T(8,128)(2,1)} %bitcast.42, bf16[384,1024]{1,0:T(8,128)(2,1)} %get-tuple-element.10.refs_1_, bf16[128,320]{1,0:T(8,128)(2,1)} %get-tuple-element.11.refs_2_, bf16[128,64]{1,0:T(8,128)(2,1)} %get-tuple-element.12.refs_3_, f32[64,256]{1,0:T(8,128)} %get-tuple-element.13.refs_4_, ...), custom_call_target="tpu_custom_call" | custom-call | bytes 1024 | tf_op jit(solution)/shard_map/pallas_call | solution.py:566
  198.0 5.2 %collective-permute-start.1 = (bf16[1,64,3584]{2,1,0:T(8,128)(2,1)}, bf16[1,64,3584]{2,1,0:T(8,128)(2,1)S(1)}, u32[]{:S(2)}, u32[]{:S(2)}) collective-permute-start(bf16[1,64,3584]{2,1,0:T(8,128)(2,1)} %bitcast.50), channel_id=1, source_target_pairs={{0,192},{64,0},{128,64},{192,128},{1,193},{65,1},{129,65},{193,129... | collective-permute-start | bytes 1376264 | tf_op jit(solution)/shard_map/ppermute | solution.py:590
  203.2 2.8 %collective-permute-done = bf16[1,64,3584]{2,1,0:T(8,128)(2,1)S(1)} collective-permute-done((bf16[1,64,3584]{2,1,0:T(8,128)(2,1)}, bf16[1,64,3584]{2,1,0:T(8,128)(2,1)S(1)}, u32[]{:S(2)}, u32[]{:S(2)}) %collective-permute-start) | collective-permute-done | bytes 458784 | tf_op jit(solution)/shard_map/ppermute | solution.py:590
  206.0 15.8 %collective-permute-done.1 = bf16[1,64,3584]{2,1,0:T(8,128)(2,1)S(1)} collective-permute-done((bf16[1,64,3584]{2,1,0:T(8,128)(2,1)}, bf16[1,64,3584]{2,1,0:T(8,128)(2,1)S(1)}, u32[]{:S(2)}, u32[]{:S(2)}) %collective-permute-start.1) | collective-permute-done | bytes 458784 | tf_op jit(solution)/shard_map/ppermute | solution.py:590
  221.8 0.8 copy.43
  222.5 0.8 copy.44
  (4 shorter events, 0.1 us)
Async XLA Ops:
  112.4 36.5 %all-to-all-start.1 = ((bf16[64,16,1152]{2,1,0:T(8,128)(2,1)}), bf16[64,16,1152]{2,1,0:T(8,128)(2,1)S(1)}, u32[]{:S(2)}, u32[]{:S(2)}) async-start(bf16[64,16,1152]{2,1,0:T(8,128)(2,1)} %bitcast.34), calls=%async_computation.1 | async-start | bytes 4718592 | tf_op jit(solution)/shard_map/all_to_all | solution.py:585
  132.5 22.8 %copy-start.6 = (f32[1,3584]{1,0:T(1,128)S(1)}, f32[1,3584]{1,0:T(1,128)}, u32[]{:S(2)}) copy-start(f32[1,3584]{1,0:T(1,128)} %refs_9_.1) | copy-start | bytes 43012
  132.5 22.8 %copy-start.2 = (bf16[1,64,3584]{2,1,0:T(8,128)(2,1)S(1)}, bf16[1,64,3584]{2,1,0:T(8,128)(2,1)}, u32[]{:S(2)}) copy-start(bf16[1,64,3584]{2,1,0:T(8,128)(2,1)} %param.14) | copy-start | bytes 1376260
  132.5 23.0 %copy-start.5 = (bf16[1,3584,32]{1,2,0:T(8,128)(2,1)S(1)}, bf16[1,3584,32]{1,2,0:T(8,128)(2,1)}, u32[]{:S(2)}) copy-start(bf16[1,3584,32]{1,2,0:T(8,128)(2,1)} %param.18) | copy-start | bytes 688132
  132.6 23.8 %copy-start.7 = (s32[1,64,2]{1,2,0:T(2,128)S(1)}, s32[1,64,2]{1,2,0:T(2,128)}, u32[]{:S(2)}) copy-start(s32[1,64,2]{1,2,0:T(2,128)} %param.16) | copy-start | bytes 1540
  132.6 23.9 %copy-start.3 = (bf16[1,64,3584]{2,1,0:T(8,128)(2,1)S(1)}, bf16[1,64,3584]{2,1,0:T(8,128)(2,1)}, u32[]{:S(2)}) copy-start(bf16[1,64,3584]{2,1,0:T(8,128)(2,1)} %param.12) | copy-start | bytes 1376260
  148.9 1.4 copy-start.1
  150.3 40.1 %all-to-all-start.2 = ((bf16[64,16,1152]{2,1,0:T(8,128)(2,1)}), bf16[64,16,1152]{2,1,0:T(8,128)(2,1)S(1)}, u32[]{:S(2)}, u32[]{:S(2)}) async-start(bf16[64,16,1152]{2,1,0:T(8,128)(2,1)} %bitcast.41), calls=%async_computation.2 | async-start | bytes 4718592 | tf_op jit(solution)/shard_map/all_to_all | solution.py:585
  156.5 33.9 %copy-start.4 = (f32[64,2]{1,0:T(8,128)}, f32[64,2]{1,0:T(8,128)S(1)}, u32[]{:S(2)}) copy-start(f32[64,2]{1,0:T(8,128)S(1)} %copy.35.refs_8_) | copy-start | bytes 1540
  167.1 38.9 %collective-permute-start = (bf16[1,64,3584]{2,1,0:T(8,128)(2,1)}, bf16[1,64,3584]{2,1,0:T(8,128)(2,1)S(1)}, u32[]{:S(2)}, u32[]{:S(2)}) collective-permute-start(bf16[1,64,3584]{2,1,0:T(8,128)(2,1)} %bitcast.51), channel_id=1, source_target_pairs={{0,64},{64,128},{128,192},{192,0},{1,65},{65,129},{129,193},{193,1... | collective-permute-start | bytes 1376264 | tf_op jit(solution)/shard_map/ppermute | solution.py:590
  190.4 1.4 copy-start
  198.0 23.7 %collective-permute-start.1 = (bf16[1,64,3584]{2,1,0:T(8,128)(2,1)}, bf16[1,64,3584]{2,1,0:T(8,128)(2,1)S(1)}, u32[]{:S(2)}, u32[]{:S(2)}) collective-permute-start(bf16[1,64,3584]{2,1,0:T(8,128)(2,1)} %bitcast.50), channel_id=1, source_target_pairs={{0,192},{64,0},{128,64},{192,128},{1,193},{65,1},{129,65},{193,129... | collective-permute-start | bytes 1376264 | tf_op jit(solution)/shard_map/ppermute | solution.py:590

commit v3 on v2

--- a/solution.py
+++ b/solution.py
@@ -63,6 +63,12 @@
     return jnp.sum(jnp.where(hit, column, 0.0), axis=0, keepdims=True)
 
 
+def as_column(row):
+    shape = (row.shape[1], row.shape[1])
+    hit = lax.broadcasted_iota(jnp.int32, shape, 0) == lax.broadcasted_iota(jnp.int32, shape, 1)
+    return jnp.sum(jnp.where(hit, row, 0.0), axis=1, keepdims=True)
+
+
 def pack(units, gain, routes):
     n, m = len(units), len(routes)
     tokens, width = units[0][0].shape
@@ -72,7 +78,7 @@
     def kernel(*refs):
         far, out = refs[: n + m + 1], refs[n + m + 1]
         near = refs[n + m + 2 : 2 * (n + m) + 3]
-        made, low, high, sems = refs[2 * (n + m) + 3 :]
+        made, stacked, sems = refs[2 * (n + m) + 3 :]
         loads = [
             pltpu.make_async_copy(src, dst, sems.at[i]) for i, (src, dst) in enumerate(zip(far, near))
         ]
@@ -81,35 +87,31 @@
         for load in loads[: m + 1]:
             load.wait()
         gain_ref = near[m]
-        shape = (half_rows, 2 * tokens)
+        shape = (half_rows, 4 * tokens)
         expert, row, block, slot = place_of(lax.broadcasted_iota(jnp.int32, shape, 0))
-        right = lax.broadcasted_iota(jnp.int32, shape, 1) >= tokens
+        lane = lax.broadcasted_iota(jnp.int32, shape, 1)
+        body_lanes = (lane < 3 * tokens) & (block == lax.shift_right_logical(lane, 6))
+        tail_lanes = (row == 15) & (lane == 3 * tokens + expert)
+        place = lax.broadcasted_iota(jnp.int32, (32 * CAP, tokens), 0)
+        tail_key = lax.bitwise_and(place, 31) * 8 + lax.shift_right_logical(place, 5)
         stores = []
+        stacked[3 * tokens :, :] = jnp.zeros((tokens, LANES), jnp.bfloat16)
         for route in range(m):
             ids = f32(near[route][...])
-            first, second = ids[:, 0:1], ids[:, 1:2]
-            first_r, second_r = as_row(first, 2), as_row(second, 2)
-            square = (tokens, 2 * tokens)
-            lane = lax.bitwise_and(lax.broadcasted_iota(jnp.int32, square, 1), tokens - 1)
-            before = lax.broadcasted_iota(jnp.int32, square, 0) < lane
+            first, second = as_column(ids[0:1, :]), as_column(ids[1:2, :])
+            first_r, second_r = as_row(first, 4), as_row(second, 4)
+            square = (tokens, 4 * tokens)
+            other = lax.bitwise_and(lax.broadcasted_iota(jnp.int32, square, 1), tokens - 1)
+            before = lax.broadcasted_iota(jnp.int32, square, 0) < other
             slot_0 = count((first == first_r) & before, 0)
             slot_1 = count(first == second_r, 0) + count((second == second_r) & before, 0)
             key_0, key_1 = first_r * 8 + slot_0, second_r * 8 + slot_1
-
-            def hits(key, key_0=key_0, key_1=key_1):
-                key = f32(key)
-                return (key_0 == key) | (key_1 == key)
-
-            def matrix(mask):
-                return jnp.where(mask, 1.0, 0.0).astype(jnp.bfloat16)
-
-            own = hits(expert * 8 + slot)
-            pick_low = matrix(own & (block == jnp.where(right, 1, 0)))
-            third = own & (block == 2) & ~right
-            pick_rest = matrix(third)
-            picks = [
-                matrix(third | (hits(expert * 8 + s) & (row == 15) & right)) for s in range(CAP)
-            ]
+            key = f32(expert * 8 + slot)
+            own = ((key_0 == key) | (key_1 == key)) & body_lanes
+            pick = jnp.where(own | tail_lanes, 1.0, 0.0).astype(jnp.bfloat16)
+            key = f32(tail_key)
+            hit = (key_0[:, :tokens] == key) | (key_1[:, :tokens] == key)
+            pick_tail = jnp.where(hit, 1.0, 0.0).astype(jnp.bfloat16)
             for u in range(n):
                 if units[u][2] != route:
                     continue
@@ -119,23 +121,22 @@
                     v = f32(x)
                     inverse = lax.rsqrt(jnp.mean(v * v, axis=-1, keepdims=True) + epsilon)
                     x = (v * inverse * gain_ref[...]).astype(jnp.bfloat16)
-                low[0:tokens, :] = x[:, :LANES]
-                low[tokens:, :] = x[:, LANES : 2 * LANES]
-                high[0:tokens, :] = x[:, 2 * LANES : TAIL]
-                high[tokens:, :] = jnp.zeros((tokens, LANES), jnp.bfloat16)
+                for g in range(3):
+                    stacked[tokens * g : tokens * g + tokens, :] = x[:, g * LANES : (g + 1) * LANES]
+                tail = jnp.dot(
+                    pick_tail, x[:, TAIL:], preferred_element_type=jnp.float32
+                ).astype(jnp.bfloat16)
                 for s in range(CAP):
-                    high[tokens:, 128 * s : 128 * s + 128] = x[:, TAIL:]
-                for s in range(9):
-                    cols = slice(128 * s, 128 * s + 128)
-                    part = jnp.dot(pick_low, low[:, cols], preferred_element_type=jnp.float32)
-                    part += jnp.dot(
-                        picks[s] if s < CAP else pick_rest,
-                        high[:, cols],
+                    stacked[3 * tokens : 3 * tokens + 32, 128 * s : 128 * s + 128] = tail[
+                        32 * s : 32 * s + 32
+                    ]
+                for c in range(3):
+                    at = u * LANES + 384 * c
+                    made[:, at : at + 384] = jnp.dot(
+                        pick,
+                        stacked[:, 384 * c : 384 * c + 384],
                         preferred_element_type=jnp.float32,
-                    )
-                    made[:, u * LANES + 128 * s : u * LANES + 128 * s + 128] = part.astype(
-                        jnp.bfloat16
-                    )
+                    ).astype(jnp.bfloat16)
                 lanes = pl.ds(u * LANES, LANES)
                 for r in range(2):
                     stores.append(
@@ -157,8 +158,7 @@
         scratch_shapes=[pltpu.VMEM(v.shape, v.dtype) for v in operands]
         + [
             pltpu.VMEM((half_rows, n * LANES), jnp.bfloat16),
-            pltpu.VMEM((2 * tokens, LANES), jnp.bfloat16),
-            pltpu.VMEM((2 * tokens, LANES), jnp.bfloat16),
+            pltpu.VMEM((4 * tokens, LANES), jnp.bfloat16),
             pltpu.SemaphoreType.DMA((3 * n + m + 1,)),
         ],
         **params(),
@@ -188,7 +188,7 @@
     ).astype(jnp.bfloat16)
 
 
-def repack(chunks, offset, tables, made, rest, extra=None):
+def repack(chunks, offset, tables, made, rest, extra=None, stores=()):
     gather, expand = tables
     tail = jnp.dot(
         expand[320:640, :], rest[...], preferred_element_type=jnp.float32
@@ -210,6 +210,10 @@
         chunks[held, offset : offset + LANES] = jnp.dot(
             gather[256:, :], made[held, :], preferred_element_type=jnp.float32
         ).astype(jnp.bfloat16)
+        if stores:
+            stores[b].start()
+    for store in stores:
+        store.wait()
 
 
 def put_result(made, rest, product):
@@ -267,10 +271,13 @@
             rest,
             lambda cols: jnp.dot(hidden[...], wd[:, cols], preferred_element_type=jnp.float32),
         )
-        repack(near, 0, tables, made, rest)
-        store = pltpu.make_async_copy(near, far_out, sems.at[8])
-        store.start()
-        store.wait()
+        stores = [
+            pltpu.make_async_copy(
+                near.at[pl.ds(256 * b, 256)], far_out.at[pl.ds(256 * b, 256)], sems.at[8 + b]
+            )
+            for b in range(4)
+        ]
+        repack(near, 0, tables, made, rest, stores=stores)
 
     rows = chunks.shape[0]
     return pl.pallas_call(
@@ -287,7 +294,7 @@
             pltpu.VMEM((320, 128), jnp.bfloat16),
             pltpu.VMEM((64, LANES), jnp.bfloat16),
             pltpu.VMEM((320, 128), jnp.bfloat16),
-            pltpu.SemaphoreType.DMA((9,)),
+            pltpu.SemaphoreType.DMA((12,)),
         ],
         **params(),
     )(chunks, *tables, *weights)
@@ -378,7 +385,7 @@
 
 
 def spread_weights(weights, routes):
-    tokens = routes[0].shape[0]
+    tokens = routes[0].shape[1]
     total_rows = 64 * ROWS
     n = len(routes)
 
@@ -394,8 +401,8 @@
         place = lax.bitwise_and(place, 31) * 8 + lax.shift_right_logical(place, 6)
         for at in range(n):
             w, ids = w_refs[at], f32(id_refs[at][...])
-            first, second = ids[:, 0:1], ids[:, 1:2]
-            first_r, second_r = as_row(first, 1), as_row(second, 1)
+            first_r, second_r = ids[0:1, :], ids[1:2, :]
+            first, second = as_column(first_r), as_column(second_r)
             slot_0 = count((first == first_r) & before, 1)
             slot_1 = count(second == first_r, 1) + count((second == second_r) & before, 1)
             key_0, key_1 = first * 8 + slot_0, second * 8 + slot_1
@@ -468,55 +475,56 @@
 
 def finish_forward(chunks, parts, tails, rows):
     tokens, width = rows.shape
-    operands = [chunks, parts, tails, rows]
-
-    def kernel(*refs):
-        out, held, result, stacked, sems = refs[4], refs[5:9], refs[9], refs[10], refs[11]
-        near, parts, tails, v = held
-        loads = load_all(refs[:4], held, sems)
+    operands = [parts, tails, rows]
+
+    def kernel(near, *refs):
+        out, held, result, stacked, sems = refs[3], refs[4:7], refs[7], refs[8], refs[9]
+        parts, tails, v = held
+        loads = load_all(refs[:3], held, sems)
         for load in loads:
             load.start()
+        rows_15 = last_rows(near, 640)
         for load in loads:
             load.wait()
 
         def put(at, size, value):
             result[:, at : at + size] = (f32(v[:, at : at + size]) + value).astype(jnp.bfloat16)
 
-        add_up(near, last_rows(near, 640), stacked, parts, tails, put)
-        store = pltpu.make_async_copy(result, out, sems.at[4])
+        add_up(near, rows_15, stacked, parts, tails, put)
+        store = pltpu.make_async_copy(result, out, sems.at[3])
         store.start()
         store.wait()
 
     return pl.pallas_call(
         kernel,
         out_shape=jax.ShapeDtypeStruct((tokens, width), jnp.bfloat16),
-        in_specs=[FAR] * 4,
+        in_specs=[NEAR] + [FAR] * 3,
         out_specs=FAR,
         scratch_shapes=[pltpu.VMEM(v.shape, v.dtype) for v in operands]
         + [
             pltpu.VMEM((tokens, width), jnp.bfloat16),
             pltpu.VMEM((64 * CAP, 128), jnp.bfloat16),
-            pltpu.SemaphoreType.DMA((5,)),
+            pltpu.SemaphoreType.DMA((4,)),
         ],
         **params(),
-    )(*operands)
+    )(chunks, *operands)
 
 
 def finish_backward(chunks, spreads, rows, cotangent, routes, picked, gain, router_rows):
     tokens, width = rows.shape
-    operands = [chunks, *spreads, rows, cotangent, routes, picked, gain, router_rows]
+    operands = [*spreads, rows, cotangent, routes, picked, gain, router_rows]
     n = len(operands)
 
-    def kernel(*refs):
+    def kernel(near, *refs):
         out, held = refs[n], refs[n + 1 : 2 * n + 1]
         gradient, total, stacked, sems = refs[2 * n + 1 :]
-        near, parts, tails, picks, slots, v_ref, cot, ids, chosen, gain_ref, router_ref = held
+        parts, tails, picks, slots, v_ref, cot, ids, chosen, gain_ref, router_ref = held
         loads = load_all(refs[:n], held, sems)
         for load in loads:
             load.start()
+        rows_15 = last_rows(near, 768)
         for load in loads:
             load.wait()
-        rows_15 = last_rows(near, 768)
         found = jnp.dot(picks[...], rows_15[:, 640:], preferred_element_type=jnp.float32)
         lane = f32(lax.broadcasted_iota(jnp.int32, (tokens, 128), 1))
         inner = [
@@ -535,10 +543,11 @@
         whole = scores[0] + scores[1]
         mean = (inner[0] * scores[0] + inner[1] * scores[1]) / whole
         numbers = f32(ids[...])
+        numbers = [as_column(numbers[k : k + 1, :]) for k in range(2)]
         d_logits = jnp.zeros((tokens, 128), jnp.float32)
         for k in range(2):
             d_logit = (inner[k] - mean) / whole * scores[k] * (1.0 - scores[k])
-            d_logits += jnp.where(lane == numbers[:, k : k + 1], d_logit, 0.0)
+            d_logits += jnp.where(lane == numbers[k], d_logit, 0.0)
         pieces, left = [], d_logits
         for _ in range(3):
             pieces.append(left.astype(jnp.bfloat16))
@@ -566,7 +575,7 @@
     return pl.pallas_call(
         kernel,
         out_shape=jax.ShapeDtypeStruct((tokens, width), jnp.bfloat16),
-        in_specs=[FAR] * n,
+        in_specs=[NEAR] + [FAR] * n,
         out_specs=FAR,
         scratch_shapes=[pltpu.VMEM(v.shape, v.dtype) for v in operands]
         + [
@@ -576,7 +585,7 @@
             pltpu.SemaphoreType.DMA((n + 1,)),
         ],
         **params(),
-    )(*operands)
+    )(chunks, *operands)
 
 
 def swapped(chunks):
@@ -621,31 +630,33 @@
     tables = selections()
     backward_ids, forward_ids = backward_routes[0], forward_routes[0]
 
+    backward_names, forward_names = backward_ids.T, forward_ids.T
     saved, cotan, forward = saved_rows[0], cotangent[0], forward_rows[0]
 
     sent = pack(
         [(saved, True, 0), (cotan, False, 0), (forward, True, 1)],
         norm_gain,
-        [backward_ids, forward_ids],
+        [backward_names, forward_names],
     )
     received = swapped(sent)
     backward_scores = picked_scores(saved, gain_row, router_map, backward_ids)
     forward_scores = picked_scores(forward, gain_row, router_map, forward_ids)
     spreads = spread_weights(
         [v / jnp.sum(v, axis=1, keepdims=True) for v in (forward_scores, backward_scores)],
-        [forward_ids, backward_ids],
+        [forward_names, backward_names],
     )
     forward_chunks = experts_forward(received, 2 * LANES, tables, weights)
     backward_chunks = experts_backward(received, tables, weights, forward_chunks)
     forward_back, backward_back = swapped(forward_chunks), swapped(backward_chunks)
     router_rows = jnp.pad(router_map.T, ((0, 128 - router_map.shape[1]), (0, 0)))
     result = finish_forward(forward_back, spreads[0], spreads[1], forward)
+    result, _ = lax.optimization_barrier((result, backward_back))
     gradient = finish_backward(
         backward_back,
         spreads[2:],
         saved,
         cotan,
-        backward_ids,
+        backward_names,
         backward_scores,
         norm_gain,
         router_rows,

time: 225 us -> 218 us (0.969)
  local copies, waits for them, and re-layouts: 8.33 us -> 2.78 us
  waiting for transfers between devices: 54.9 us -> 58.2 us
  starting transfers between devices: 18.2 us -> 15.2 us
    ppermute x2, waiting for transfers between devices: 18.5 us -> 22 us  [passed_along(): return lax.ppermute(x, axis, [(i, (i + by) % n) for i in range(n)])]
    ppermute x2, starting transfers between devices: 8.5 us -> 5.23 us  [passed_along(): return lax.ppermute(x, axis, [(i, (i + by) % n) for i in range(n)])]
    unnamed x18, local copies, waits for them, and re-layouts: 4.39 us -> 1.58 us
    squeeze x2 -> x0, local copies, waits for them, and re-layouts: 2.75 us -> none  [body(): backward_ids, forward_ids = (backward_routes[0], forward_routes[0])]
  transfers between devices with their start and end apart: 4 -> 4, of which waited for: 4 -> 4; matrix products, arithmetic and copies ran while one was open for 2% -> 2% of each run, Pallas kernels for 13% -> 14%
where the time goes in v3:
time: 218 us; the launch traced here: 217 us
  blocking collectives  93 us (43%)
  waiting for transfers between devices  58.2 us (27%)
  Pallas kernels  44.4 us (20%)
  starting transfers between devices  15.2 us (7%)
  local copies, waits for them, and re-layouts  2.78 us (1%)
    all_to_all x1, blocking collectives, swapped(): return lax.all_to_all(chunks, 'expert', 0, 0, tiled=True).reshape(shape)  93 us
    all_to_all x2, waiting for transfers between devices, swapped(): return lax.all_to_all(chunks, 'expert', 0, 0, tiled=True).reshape(shape)  36.2 us
    ppermute x2, waiting for transfers between devices, passed_along(): return lax.ppermute(x, axis, [(i, (i + by) % n) for i in range(n)])  22 us
    pallas_call x1, Pallas kernels, experts_backward(): pl.pallas_call(kernel, out_shape=jax.ShapeDtypeStruct((rows, LANES), jnp....  15.4 us
    all_to_all x2, starting transfers between devices, swapped(): return lax.all_to_all(chunks, 'expert', 0, 0, tiled=True).reshape(shape)  9.96 us
    pallas_call x1, Pallas kernels, experts_forward(): pl.pallas_call(kernel, out_shape=jax.ShapeDtypeStruct((rows, LANES), jnp....  9.28 us
    pallas_call x1, Pallas kernels, finish_backward(): pl.pallas_call(kernel, out_shape=jax.ShapeDtypeStruct((tokens, width), jn...  6.73 us
    pallas_call x1, Pallas kernels, pack(): pl.pallas_call(kernel, out_shape=jax.ShapeDtypeStruct((2 * half_rows, n *...  5.32 us
  transfers between devices with their start and end apart: 4, of which 4 were waited for; matrix products, arithmetic and copies ran while one was open for 2% of the time, Pallas kernels for 14%

profile of v3, /device:TPU:1, one launch (start us, length us, event | category | flops | bytes accessed | tf_op | source)
XLA Modules:
  0.0 217.2 jit_solution(4315011456646634159)
XLA Ops:
  0.6 5.3 %shard_map.131 = bf16[1024,3456]{1,0:T(8,128)(2,1)} custom-call(s32[2,64]{1,0:T(2,128)} %bitcast.56, s32[2,64]{1,0:T(2,128)} %bitcast.60, f32[1,3584]{1,0:T(1,128)} %refs_8_.1, bf16[64,3584]{1,0:T(8,128)(2,1)} %bitcast.47, bf16[64,3584]{1,0:T(8,128)(2,1)} %bitcast.51, bf16[64,3584]{1,0:T(8,128)(2,1)} %bitcast.49), custom_call_target="tpu_custom_call" | custom-call | bytes 1024 | tf_op jit(solution)/shard_map/pallas_call | solution.py:153
  6.0 93.0 %all_to_all.15 = bf16[64,16,3456]{2,1,0:T(8,128)(2,1)} all-to-all(bf16[64,16,3456]{2,1,0:T(8,128)(2,1)} %bitcast.37), channel_id=1, replica_groups=mesh['pipe'=4,'expert'=64] {'expert'}, dimensions={0} | all-to-all | bytes 14155776 | tf_op jit(solution)/shard_map/all_to_all | solution.py:594
  99.0 9.3 %shard_map.132.refs_5_ = bf16[1024,1152]{1,0:T(8,128)(2,1)} custom-call(bf16[1024,3456]{1,0:T(8,128)(2,1)} %bitcast.35, bf16[512,256]{1,0:T(8,128)(2,1)} %constant.19.clone.refs_0_, bf16[704,320]{1,0:T(8,128)(2,1)} %constant.20.clone.refs_1_, bf16[3584,512]{1,0:T(8,128)(2,1)} %bitcast.39, bf16[3584,512]{1,0:T(8,128)(2,1)} %bitcast.41, bf16[512,3584]{1,0:T(8,128)(2,1)} %bitcast.43), custom_call_target="tpu_custom_call" | custom-call | bytes 1024 | tf_op jit(solution)/shard_map/pallas_call | solution.py:283
  108.3 4.7 %all-to-all-start.1 = ((bf16[64,16,1152]{2,1,0:T(8,128)(2,1)}), bf16[64,16,1152]{2,1,0:T(8,128)(2,1)S(1)}, u32[]{:S(2)}, u32[]{:S(2)}) async-start(bf16[64,16,1152]{2,1,0:T(8,128)(2,1)} %bitcast.38), calls=%async_computation.1 | async-start | bytes 4718592 | tf_op jit(solution)/shard_map/all_to_all | solution.py:594
  113.0 15.4 %shard_map.135 = bf16[1024,1152]{1,0:T(8,128)(2,1)} custom-call(bf16[1024,3456]{1,0:T(8,128)(2,1)} %bitcast.36, bf16[512,256]{1,0:T(8,128)(2,1)} %constant.19.clone.refs_0_, bf16[704,320]{1,0:T(8,128)(2,1)} %constant.20.clone.refs_1_, bf16[3584,512]{1,0:T(8,128)(2,1)} %bitcast.40, bf16[3584,512]{1,0:T(8,128)(2,1)} %bitcast.42, bf16[512,3584]{1,0:T(8,128)(2,1)} %bitcast.44, ...), custom_call_target="tpu_custom_call" | custom-call | bytes 1024 | tf_op jit(solution)/shard_map/pallas_call | solution.py:364
  128.4 0.0 copy-start.5
  128.4 0.0 copy-start.1
  128.4 0.0 copy-start.4
  128.4 0.0 copy-start.6
  128.5 0.0 copy-start.2
  128.5 16.3 %all-to-all-done.1 = bf16[64,16,1152]{2,1,0:T(8,128)(2,1)S(1)} async-done(((bf16[64,16,1152]{2,1,0:T(8,128)(2,1)}), bf16[64,16,1152]{2,1,0:T(8,128)(2,1)S(1)}, u32[]{:S(2)}, u32[]{:S(2)}) %all-to-all-start.1) | async-done | bytes 2359328 | tf_op jit(solution)/shard_map/all_to_all | solution.py:594
  144.8 0.0 copy-start
  144.8 0.0 copy-start.7
  144.8 5.3 %all-to-all-start.2 = ((bf16[64,16,1152]{2,1,0:T(8,128)(2,1)}), bf16[64,16,1152]{2,1,0:T(8,128)(2,1)}, u32[]{:S(2)}, u32[]{:S(2)}) async-start(bf16[64,16,1152]{2,1,0:T(8,128)(2,1)} %bitcast.45), calls=%async_computation.2 | async-start | bytes 4718592 | tf_op jit(solution)/shard_map/all_to_all | solution.py:594
  150.0 0.0 copy-done.5
  150.1 0.0 copy-done.1
  150.1 0.2 multiply_reduce_fusion
  150.3 0.0 copy-done.4
  150.3 0.8 fusion.2
  151.1 0.0 copy-done.6
  151.1 0.1 copy.23.refs_7_
  151.2 0.0 copy-done.2
  151.2 0.0 copy-start.3
  151.2 0.2 multiply_reduce_fusion.1
  151.5 0.8 fusion.5
  152.2 0.0 copy-done
  152.2 0.0 copy-done.7
  152.3 0.1 copy.21
  152.4 0.7 broadcast_divide_fusion
  153.1 2.5 %shard_map.133 = (bf16[384,1024]{1,0:T(8,128)(2,1)}, bf16[128,320]{1,0:T(8,128)(2,1)}, bf16[384,1024]{1,0:T(8,128)(2,1)}, bf16[128,320]{1,0:T(8,128)(2,1)}, bf16[128,64]{1,0:T(8,128)(2,1)}, /*index=5*/f32[64,256]{1,0:T(8,128)}) custom-call(f32[64,2]{1,0:T(8,128)} %get-tuple-element.21.refs_0_, f32[64,2]{1,0:T(8,128)} %get-tuple-element.20.refs_1_, ...), custom_call_target="tpu_custom_call" | custom-call | bytes 1024 | tf_op jit(solution)/shard_map/pallas_call | solution.py:438
  155.6 1.0 pad.4.refs_9_
  156.6 5.2 %shard_map.134 = bf16[64,3584]{1,0:T(8,128)(2,1)} custom-call(bf16[1024,1152]{1,0:T(8,128)(2,1)} %bitcast.46, bf16[384,1024]{1,0:T(8,128)(2,1)} %get-tuple-element.9.refs_0_, bf16[128,320]{1,0:T(8,128)(2,1)} %get-tuple-element.10.refs_1_, bf16[64,3584]{1,0:T(8,128)(2,1)} %bitcast.50), custom_call_target="tpu_custom_call" | custom-call | bytes 1024 | tf_op jit(solution)/shard_map/pallas_call | solution.py:498
  161.8 19.9 %all-to-all-done.2 = bf16[64,16,1152]{2,1,0:T(8,128)(2,1)} async-done(((bf16[64,16,1152]{2,1,0:T(8,128)(2,1)}), bf16[64,16,1152]{2,1,0:T(8,128)(2,1)}, u32[]{:S(2)}, u32[]{:S(2)}) %all-to-all-start.2) | async-done | bytes 2359328 | tf_op jit(solution)/shard_map/all_to_all | solution.py:594
  181.8 3.0 %collective-permute-start = (bf16[1,64,3584]{2,1,0:T(8,128)(2,1)}, bf16[1,64,3584]{2,1,0:T(8,128)(2,1)S(1)}, u32[]{:S(2)}, u32[]{:S(2)}) collective-permute-start(bf16[1,64,3584]{2,1,0:T(8,128)(2,1)} %bitcast.54), channel_id=1, source_target_pairs={{0,64},{64,128},{128,192},{192,0},{1,65},{65,129},{129,193},{193,1... | collective-permute-start | bytes 1376264 | tf_op jit(solution)/shard_map/ppermute | solution.py:599
  184.8 0.0 copy-done.3
  184.8 6.7 %shard_map.136 = bf16[64,3584]{1,0:T(8,128)(2,1)} custom-call(bf16[1024,1152]{1,0:T(8,128)(2,1)} %bitcast.20.near, bf16[384,1024]{1,0:T(8,128)(2,1)} %get-tuple-element.12.refs_0_, bf16[128,320]{1,0:T(8,128)(2,1)} %get-tuple-element.13.refs_1_, bf16[128,64]{1,0:T(8,128)(2,1)} %get-tuple-element.14.refs_2_, f32[64,256]{1,0:T(8,128)} %get-tuple-element.15.refs_3_, ...), custom_call_target="tpu_custom_call" | custom-call | bytes 1024 | tf_op jit(solution)/shard_map/pallas_call | solution.py:575
  191.5 2.2 %collective-permute-start.1 = (bf16[1,64,3584]{2,1,0:T(8,128)(2,1)}, bf16[1,64,3584]{2,1,0:T(8,128)(2,1)S(1)}, u32[]{:S(2)}, u32[]{:S(2)}) collective-permute-start(bf16[1,64,3584]{2,1,0:T(8,128)(2,1)} %bitcast.53), channel_id=1, source_target_pairs={{0,192},{64,0},{128,64},{192,128},{1,193},{65,1},{129,65},{193,129... | collective-permute-start | bytes 1376264 | tf_op jit(solution)/shard_map/ppermute | solution.py:599
  193.7 10.6 %collective-permute-done = bf16[1,64,3584]{2,1,0:T(8,128)(2,1)S(1)} collective-permute-done((bf16[1,64,3584]{2,1,0:T(8,128)(2,1)}, bf16[1,64,3584]{2,1,0:T(8,128)(2,1)S(1)}, u32[]{:S(2)}, u32[]{:S(2)}) %collective-permute-start) | collective-permute-done | bytes 458784 | tf_op jit(solution)/shard_map/ppermute | solution.py:599
  204.3 11.4 %collective-permute-done.1 = bf16[1,64,3584]{2,1,0:T(8,128)(2,1)S(1)} collective-permute-done((bf16[1,64,3584]{2,1,0:T(8,128)(2,1)}, bf16[1,64,3584]{2,1,0:T(8,128)(2,1)S(1)}, u32[]{:S(2)}, u32[]{:S(2)}) %collective-permute-start.1) | collective-permute-done | bytes 458784 | tf_op jit(solution)/shard_map/ppermute | solution.py:599
  215.7 0.8 copy.28
  216.4 0.8 copy.29
  (5 shorter events, 0.1 us)
Async XLA Ops:
  108.3 36.5 %all-to-all-start.1 = ((bf16[64,16,1152]{2,1,0:T(8,128)(2,1)}), bf16[64,16,1152]{2,1,0:T(8,128)(2,1)S(1)}, u32[]{:S(2)}, u32[]{:S(2)}) async-start(bf16[64,16,1152]{2,1,0:T(8,128)(2,1)} %bitcast.38), calls=%async_computation.1 | async-start | bytes 4718592 | tf_op jit(solution)/shard_map/all_to_all | solution.py:594
  128.4 21.6 %copy-start.5 = (f32[1,3584]{1,0:T(1,128)S(1)}, f32[1,3584]{1,0:T(1,128)}, u32[]{:S(2)}) copy-start(f32[1,3584]{1,0:T(1,128)} %refs_8_.1) | copy-start | bytes 43012
  128.4 21.7 %copy-start.1 = (bf16[1,64,3584]{2,1,0:T(8,128)(2,1)S(1)}, bf16[1,64,3584]{2,1,0:T(8,128)(2,1)}, u32[]{:S(2)}) copy-start(bf16[1,64,3584]{2,1,0:T(8,128)(2,1)} %param.14) | copy-start | bytes 1376260
  128.4 21.9 %copy-start.4 = (bf16[1,3584,32]{1,2,0:T(8,128)(2,1)S(1)}, bf16[1,3584,32]{1,2,0:T(8,128)(2,1)}, u32[]{:S(2)}) copy-start(bf16[1,3584,32]{1,2,0:T(8,128)(2,1)} %param.18) | copy-start | bytes 688132
  128.4 22.7 %copy-start.6 = (s32[1,64,2]{1,2,0:T(2,128)S(1)}, s32[1,64,2]{1,2,0:T(2,128)}, u32[]{:S(2)}) copy-start(s32[1,64,2]{1,2,0:T(2,128)} %param.16) | copy-start | bytes 1540
  128.5 22.8 %copy-start.2 = (bf16[1,64,3584]{2,1,0:T(8,128)(2,1)S(1)}, bf16[1,64,3584]{2,1,0:T(8,128)(2,1)}, u32[]{:S(2)}) copy-start(bf16[1,64,3584]{2,1,0:T(8,128)(2,1)} %param.12) | copy-start | bytes 1376260
  144.8 7.5 %copy-start = (bf16[64,16,1152]{2,1,0:T(8,128)(2,1)}, bf16[64,16,1152]{2,1,0:T(8,128)(2,1)S(1)}, u32[]{:S(2)}) copy-start(bf16[64,16,1152]{2,1,0:T(8,128)(2,1)S(1)} %all-to-all-done.1) | copy-start | bytes 7077892
  144.8 7.5 %copy-start.7 = (s32[1,64,2]{1,2,0:T(2,128)S(1)}, s32[1,64,2]{1,2,0:T(2,128)}, u32[]{:S(2)}) copy-start(s32[1,64,2]{1,2,0:T(2,128)} %param.13) | copy-start | bytes 1540
  144.8 37.0 %all-to-all-start.2 = ((bf16[64,16,1152]{2,1,0:T(8,128)(2,1)}), bf16[64,16,1152]{2,1,0:T(8,128)(2,1)}, u32[]{:S(2)}, u32[]{:S(2)}) async-start(bf16[64,16,1152]{2,1,0:T(8,128)(2,1)} %bitcast.45), calls=%async_computation.2 | async-start | bytes 4718592 | tf_op jit(solution)/shard_map/all_to_all | solution.py:594
  151.2 33.5 %copy-start.3 = (f32[64,2]{1,0:T(8,128)}, f32[64,2]{1,0:T(8,128)S(1)}, u32[]{:S(2)}) copy-start(f32[64,2]{1,0:T(8,128)S(1)} %copy.23.refs_7_) | copy-start | bytes 1540
  181.8 22.5 %collective-permute-start = (bf16[1,64,3584]{2,1,0:T(8,128)(2,1)}, bf16[1,64,3584]{2,1,0:T(8,128)(2,1)S(1)}, u32[]{:S(2)}, u32[]{:S(2)}) collective-permute-start(bf16[1,64,3584]{2,1,0:T(8,128)(2,1)} %bitcast.54), channel_id=1, source_target_pairs={{0,64},{64,128},{128,192},{192,0},{1,65},{65,129},{129,193},{193,1... | collective-permute-start | bytes 1376264 | tf_op jit(solution)/shard_map/ppermute | solution.py:599
  191.5 24.2 %collective-permute-start.1 = (bf16[1,64,3584]{2,1,0:T(8,128)(2,1)}, bf16[1,64,3584]{2,1,0:T(8,128)(2,1)S(1)}, u32[]{:S(2)}, u32[]{:S(2)}) collective-permute-start(bf16[1,64,3584]{2,1,0:T(8,128)(2,1)} %bitcast.53), channel_id=1, source_target_pairs={{0,192},{64,0},{128,64},{192,128},{1,193},{65,1},{129,65},{193,129... | collective-permute-start | bytes 1376264 | tf_op jit(solution)/shard_map/ppermute | solution.py:599

commit v4 on v3

--- a/solution.py
+++ b/solution.py
@@ -7,7 +7,7 @@
 from jax.sharding import PartitionSpec as P
 
 epsilon = 1e-06
-VMEM_LIMIT = 60 * 1024 * 1024
+VMEM_LIMIT = 63 * 1024 * 1024 + 512 * 1024
 CAP = 5
 LANES = 1152
 ROWS = 16
@@ -515,16 +515,24 @@
     operands = [*spreads, rows, cotangent, routes, picked, gain, router_rows]
     n = len(operands)
 
-    def kernel(near, *refs):
+    def kernel(far, *refs):
         out, held = refs[n], refs[n + 1 : 2 * n + 1]
-        gradient, total, stacked, sems = refs[2 * n + 1 :]
+        gradient, total, stacked, near, sems = refs[2 * n + 1 :]
         parts, tails, picks, slots, v_ref, cot, ids, chosen, gain_ref, router_ref = held
         loads = load_all(refs[:n], held, sems)
-        for load in loads:
-            load.start()
+        chunk_load = pltpu.make_async_copy(far, near, sems.at[n + 1])
+        small, large = (1, 2, 3, 4, 6, 7, 8), (9, 0, 5)
+        for i in small:
+            loads[i].start()
+        chunk_load.start()
+        for i in large:
+            loads[i].start()
+        for i in small:
+            loads[i].wait()
+        v = f32(v_ref[...])
+        inverse = lax.rsqrt(jnp.mean(v * v, axis=-1, keepdims=True) + epsilon)
+        chunk_load.wait()
         rows_15 = last_rows(near, 768)
-        for load in loads:
-            load.wait()
         found = jnp.dot(picks[...], rows_15[:, 640:], preferred_element_type=jnp.float32)
         lane = f32(lax.broadcasted_iota(jnp.int32, (tokens, 128), 1))
         inner = [
@@ -552,7 +560,9 @@
         for _ in range(3):
             pieces.append(left.astype(jnp.bfloat16))
             left = left - f32(pieces[-1])
-        pieces = jnp.concatenate(pieces, axis=0)
+        pieces = jnp.concatenate(pieces, axis=0)[:, : router_ref.shape[0]]
+        for i in large:
+            loads[i].wait()
 
         def keep(at, size, value):
             routed = jnp.dot(
@@ -564,7 +574,6 @@
 
         add_up(near, rows_15, stacked, parts, tails, keep)
         v = f32(v_ref[...])
-        inverse = lax.rsqrt(jnp.mean(v * v, axis=-1, keepdims=True) + epsilon)
         projected = jnp.mean(v * total[...], axis=-1, keepdims=True)
         d_rows = total[...] * inverse - v * (inverse * inverse * inverse * projected)
         gradient[...] = (f32(cot[...]) + d_rows).astype(jnp.bfloat16)
@@ -575,14 +584,15 @@
     return pl.pallas_call(
         kernel,
         out_shape=jax.ShapeDtypeStruct((tokens, width), jnp.bfloat16),
-        in_specs=[NEAR] + [FAR] * n,
+        in_specs=[FAR] * (n + 1),
         out_specs=FAR,
         scratch_shapes=[pltpu.VMEM(v.shape, v.dtype) for v in operands]
         + [
             pltpu.VMEM((tokens, width), jnp.bfloat16),
             pltpu.VMEM((tokens, width), jnp.float32),
             pltpu.VMEM((64 * CAP, 128), jnp.bfloat16),
-            pltpu.SemaphoreType.DMA((n + 1,)),
+            pltpu.VMEM(chunks.shape, jnp.bfloat16),
+            pltpu.SemaphoreType.DMA((n + 2,)),
         ],
         **params(),
     )(chunks, *operands)
@@ -648,7 +658,7 @@
     forward_chunks = experts_forward(received, 2 * LANES, tables, weights)
     backward_chunks = experts_backward(received, tables, weights, forward_chunks)
     forward_back, backward_back = swapped(forward_chunks), swapped(backward_chunks)
-    router_rows = jnp.pad(router_map.T, ((0, 128 - router_map.shape[1]), (0, 0)))
+    router_rows = router_map.T
     result = finish_forward(forward_back, spreads[0], spreads[1], forward)
     result, _ = lax.optimization_barrier((result, backward_back))
     gradient = finish_backward(

time: 218 us -> 218 us (level)
  transfers between devices with their start and end apart: 4 -> 4, of which waited for: 4 -> 4; matrix products, arithmetic and copies ran while one was open for 2% -> 1% of each run, Pallas kernels for 14% -> 13%
where the time goes in v4:
time: 218 us; the launch traced here: 217 us
  blocking collectives  93 us (43%)
  waiting for transfers between devices  59.2 us (27%)
  Pallas kernels  43.6 us (20%)
  starting transfers between devices  15.8 us (7%)
    all_to_all x1, blocking collectives, swapped(): return lax.all_to_all(chunks, 'expert', 0, 0, tiled=True).reshape(shape)  93 us
    all_to_all x2, waiting for transfers between devices, swapped(): return lax.all_to_all(chunks, 'expert', 0, 0, tiled=True).reshape(shape)  37.3 us
    ppermute x2, waiting for transfers between devices, passed_along(): return lax.ppermute(x, axis, [(i, (i + by) % n) for i in range(n)])  22 us
    pallas_call x1, Pallas kernels, experts_backward(): pl.pallas_call(kernel, out_shape=jax.ShapeDtypeStruct((rows, LANES), jnp....  15.4 us
    all_to_all x2, starting transfers between devices, swapped(): return lax.all_to_all(chunks, 'expert', 0, 0, tiled=True).reshape(shape)  10.6 us
    pallas_call x1, Pallas kernels, experts_forward(): pl.pallas_call(kernel, out_shape=jax.ShapeDtypeStruct((rows, LANES), jnp....  9.39 us
    pallas_call x1, Pallas kernels, finish_backward(): pl.pallas_call(kernel, out_shape=jax.ShapeDtypeStruct((tokens, width), jn...  5.74 us
    pallas_call x1, Pallas kernels, pack(): pl.pallas_call(kernel, out_shape=jax.ShapeDtypeStruct((2 * half_rows, n *...  5.32 us
  transfers between devices with their start and end apart: 4, of which 4 were waited for; matrix products, arithmetic and copies ran while one was open for 1% of the time, Pallas kernels for 13%

profile of v4, /device:TPU:1, one launch (start us, length us, event | category | flops | bytes accessed | tf_op | source)
XLA Modules:
  0.0 217.0 jit_solution(6374548141309431932)
XLA Ops:
  0.6 5.3 %shard_map.131 = bf16[1024,3456]{1,0:T(8,128)(2,1)} custom-call(s32[2,64]{1,0:T(2,128)} %bitcast.55, s32[2,64]{1,0:T(2,128)} %bitcast.59, f32[1,3584]{1,0:T(1,128)} %refs_8_.1, bf16[64,3584]{1,0:T(8,128)(2,1)} %bitcast.46, bf16[64,3584]{1,0:T(8,128)(2,1)} %bitcast.50, bf16[64,3584]{1,0:T(8,128)(2,1)} %bitcast.48), custom_call_target="tpu_custom_call" | custom-call | bytes 1024 | tf_op jit(solution)/shard_map/pallas_call | solution.py:153
  6.0 93.0 %all_to_all.15 = bf16[64,16,3456]{2,1,0:T(8,128)(2,1)} all-to-all(bf16[64,16,3456]{2,1,0:T(8,128)(2,1)} %bitcast.37), channel_id=1, replica_groups=mesh['pipe'=4,'expert'=64] {'expert'}, dimensions={0} | all-to-all | bytes 14155776 | tf_op jit(solution)/shard_map/all_to_all | solution.py:604
  99.0 9.4 %shard_map.132.refs_5_ = bf16[1024,1152]{1,0:T(8,128)(2,1)} custom-call(bf16[1024,3456]{1,0:T(8,128)(2,1)} %bitcast.35, bf16[512,256]{1,0:T(8,128)(2,1)} %constant.16.clone.refs_0_, bf16[704,320]{1,0:T(8,128)(2,1)} %constant.17.clone.refs_1_, bf16[3584,512]{1,0:T(8,128)(2,1)} %bitcast.39, bf16[3584,512]{1,0:T(8,128)(2,1)} %bitcast.41, bf16[512,3584]{1,0:T(8,128)(2,1)} %bitcast.43), custom_call_target="tpu_custom_call" | custom-call | bytes 1024 | tf_op jit(solution)/shard_map/pallas_call | solution.py:283
  108.4 5.4 %all-to-all-start.1 = ((bf16[64,16,1152]{2,1,0:T(8,128)(2,1)}), bf16[64,16,1152]{2,1,0:T(8,128)(2,1)}, u32[]{:S(2)}, u32[]{:S(2)}) async-start(bf16[64,16,1152]{2,1,0:T(8,128)(2,1)} %bitcast.38), calls=%async_computation.1 | async-start | bytes 4718592 | tf_op jit(solution)/shard_map/all_to_all | solution.py:604
  113.8 15.4 %shard_map.135 = bf16[1024,1152]{1,0:T(8,128)(2,1)} custom-call(bf16[1024,3456]{1,0:T(8,128)(2,1)} %bitcast.36, bf16[512,256]{1,0:T(8,128)(2,1)} %constant.16.clone.refs_0_, bf16[704,320]{1,0:T(8,128)(2,1)} %constant.17.clone.refs_1_, bf16[3584,512]{1,0:T(8,128)(2,1)} %bitcast.40, bf16[3584,512]{1,0:T(8,128)(2,1)} %bitcast.42, bf16[512,3584]{1,0:T(8,128)(2,1)} %bitcast.44, ...), custom_call_target="tpu_custom_call" | custom-call | bytes 1024 | tf_op jit(solution)/shard_map/pallas_call | solution.py:364
  129.2 0.0 copy-start.4
  129.2 0.0 copy-start
  129.2 0.0 copy-start.3
  129.2 0.0 copy-start.5
  129.2 0.0 copy-start.1
  129.2 16.3 %all-to-all-done.1 = bf16[64,16,1152]{2,1,0:T(8,128)(2,1)} async-done(((bf16[64,16,1152]{2,1,0:T(8,128)(2,1)}), bf16[64,16,1152]{2,1,0:T(8,128)(2,1)}, u32[]{:S(2)}, u32[]{:S(2)}) %all-to-all-start.1) | async-done | bytes 2359328 | tf_op jit(solution)/shard_map/all_to_all | solution.py:604
  145.6 0.0 copy-start.6
  145.6 5.3 %all-to-all-start.2 = ((bf16[64,16,1152]{2,1,0:T(8,128)(2,1)}), bf16[64,16,1152]{2,1,0:T(8,128)(2,1)}, u32[]{:S(2)}, u32[]{:S(2)}) async-start(bf16[64,16,1152]{2,1,0:T(8,128)(2,1)} %bitcast.45), calls=%async_computation.2 | async-start | bytes 4718592 | tf_op jit(solution)/shard_map/all_to_all | solution.py:604
  150.9 0.0 copy-done.4
  150.9 0.0 copy-done
  150.9 0.2 multiply_reduce_fusion
  151.1 0.0 copy-done.3
  151.1 0.8 fusion.2
  151.9 0.0 copy-done.5
  152.0 0.1 copy.23.refs_7_
  152.1 0.0 copy-done.1
  152.1 0.0 copy-start.2
  152.1 0.2 multiply_reduce_fusion.1
  152.3 0.8 fusion.5
  153.1 0.0 copy-done.6
  153.1 0.1 copy.21
  153.2 0.0 copy-done.2
  153.2 0.7 broadcast_divide_fusion
  153.9 2.5 %shard_map.133 = (bf16[384,1024]{1,0:T(8,128)(2,1)}, bf16[128,320]{1,0:T(8,128)(2,1)}, bf16[384,1024]{1,0:T(8,128)(2,1)}, bf16[128,320]{1,0:T(8,128)(2,1)}, bf16[128,64]{1,0:T(8,128)(2,1)}, /*index=5*/f32[64,256]{1,0:T(8,128)}) custom-call(f32[64,2]{1,0:T(8,128)} %get-tuple-element.21.refs_0_, f32[64,2]{1,0:T(8,128)} %get-tuple-element.20.refs_1_, ...), custom_call_target="tpu_custom_call" | custom-call | bytes 1024 | tf_op jit(solution)/shard_map/pallas_call | solution.py:438
  156.4 5.2 %shard_map.134 = bf16[64,3584]{1,0:T(8,128)(2,1)} custom-call(bf16[1024,1152]{1,0:T(8,128)(2,1)} %bitcast.13.near, bf16[384,1024]{1,0:T(8,128)(2,1)} %get-tuple-element.9.refs_0_, bf16[128,320]{1,0:T(8,128)(2,1)} %get-tuple-element.10.refs_1_, bf16[64,3584]{1,0:T(8,128)(2,1)} %bitcast.49), custom_call_target="tpu_custom_call" | custom-call | bytes 1024 | tf_op jit(solution)/shard_map/pallas_call | solution.py:498
  161.6 20.9 %all-to-all-done.2 = bf16[64,16,1152]{2,1,0:T(8,128)(2,1)} async-done(((bf16[64,16,1152]{2,1,0:T(8,128)(2,1)}), bf16[64,16,1152]{2,1,0:T(8,128)(2,1)}, u32[]{:S(2)}, u32[]{:S(2)}) %all-to-all-start.2) | async-done | bytes 2359328 | tf_op jit(solution)/shard_map/all_to_all | solution.py:604
  182.6 3.0 %collective-permute-start = (bf16[1,64,3584]{2,1,0:T(8,128)(2,1)}, bf16[1,64,3584]{2,1,0:T(8,128)(2,1)S(1)}, u32[]{:S(2)}, u32[]{:S(2)}) collective-permute-start(bf16[1,64,3584]{2,1,0:T(8,128)(2,1)} %bitcast.53), channel_id=1, source_target_pairs={{0,64},{64,128},{128,192},{192,0},{1,65},{65,129},{129,193},{193,1... | collective-permute-start | bytes 1376264 | tf_op jit(solution)/shard_map/ppermute | solution.py:609
  185.6 5.7 %shard_map.136 = bf16[64,3584]{1,0:T(8,128)(2,1)} custom-call(bf16[1024,1152]{1,0:T(8,128)(2,1)} %bitcast.20.far, bf16[384,1024]{1,0:T(8,128)(2,1)} %get-tuple-element.12.refs_0_, bf16[128,320]{1,0:T(8,128)(2,1)} %get-tuple-element.13.refs_1_, bf16[128,64]{1,0:T(8,128)(2,1)} %get-tuple-element.14.refs_2_, f32[64,256]{1,0:T(8,128)} %get-tuple-element.15.refs_3_, ...), custom_call_target="tpu_custom_call" | custom-call | bytes 1024 | tf_op jit(solution)/shard_map/pallas_call | solution.py:584
  191.3 2.2 %collective-permute-start.1 = (bf16[1,64,3584]{2,1,0:T(8,128)(2,1)}, bf16[1,64,3584]{2,1,0:T(8,128)(2,1)S(1)}, u32[]{:S(2)}, u32[]{:S(2)}) collective-permute-start(bf16[1,64,3584]{2,1,0:T(8,128)(2,1)} %bitcast.52), channel_id=1, source_target_pairs={{0,192},{64,0},{128,64},{192,128},{1,193},{65,1},{129,65},{193,129... | collective-permute-start | bytes 1376264 | tf_op jit(solution)/shard_map/ppermute | solution.py:609
  193.5 11.6 %collective-permute-done = bf16[1,64,3584]{2,1,0:T(8,128)(2,1)S(1)} collective-permute-done((bf16[1,64,3584]{2,1,0:T(8,128)(2,1)}, bf16[1,64,3584]{2,1,0:T(8,128)(2,1)S(1)}, u32[]{:S(2)}, u32[]{:S(2)}) %collective-permute-start) | collective-permute-done | bytes 458784 | tf_op jit(solution)/shard_map/ppermute | solution.py:609
  205.1 10.4 %collective-permute-done.1 = bf16[1,64,3584]{2,1,0:T(8,128)(2,1)S(1)} collective-permute-done((bf16[1,64,3584]{2,1,0:T(8,128)(2,1)}, bf16[1,64,3584]{2,1,0:T(8,128)(2,1)S(1)}, u32[]{:S(2)}, u32[]{:S(2)}) %collective-permute-start.1) | collective-permute-done | bytes 458784 | tf_op jit(solution)/shard_map/ppermute | solution.py:609
  215.5 0.8 copy.28
  216.3 0.8 copy.29
  (5 shorter events, 0.1 us)
Async XLA Ops:
  108.4 37.2 %all-to-all-start.1 = ((bf16[64,16,1152]{2,1,0:T(8,128)(2,1)}), bf16[64,16,1152]{2,1,0:T(8,128)(2,1)}, u32[]{:S(2)}, u32[]{:S(2)}) async-start(bf16[64,16,1152]{2,1,0:T(8,128)(2,1)} %bitcast.38), calls=%async_computation.1 | async-start | bytes 4718592 | tf_op jit(solution)/shard_map/all_to_all | solution.py:604
  129.2 21.7 %copy-start.4 = (f32[1,3584]{1,0:T(1,128)S(1)}, f32[1,3584]{1,0:T(1,128)}, u32[]{:S(2)}) copy-start(f32[1,3584]{1,0:T(1,128)} %refs_8_.1) | copy-start | bytes 43012
  129.2 21.7 %copy-start = (bf16[1,64,3584]{2,1,0:T(8,128)(2,1)S(1)}, bf16[1,64,3584]{2,1,0:T(8,128)(2,1)}, u32[]{:S(2)}) copy-start(bf16[1,64,3584]{2,1,0:T(8,128)(2,1)} %param.14) | copy-start | bytes 1376260
  129.2 21.9 %copy-start.3 = (bf16[1,3584,32]{1,2,0:T(8,128)(2,1)S(1)}, bf16[1,3584,32]{1,2,0:T(8,128)(2,1)}, u32[]{:S(2)}) copy-start(bf16[1,3584,32]{1,2,0:T(8,128)(2,1)} %param.18) | copy-start | bytes 688132
  129.2 22.7 %copy-start.5 = (s32[1,64,2]{1,2,0:T(2,128)S(1)}, s32[1,64,2]{1,2,0:T(2,128)}, u32[]{:S(2)}) copy-start(s32[1,64,2]{1,2,0:T(2,128)} %param.16) | copy-start | bytes 1540
  129.2 22.8 %copy-start.1 = (bf16[1,64,3584]{2,1,0:T(8,128)(2,1)S(1)}, bf16[1,64,3584]{2,1,0:T(8,128)(2,1)}, u32[]{:S(2)}) copy-start(bf16[1,64,3584]{2,1,0:T(8,128)(2,1)} %param.12) | copy-start | bytes 1376260
  145.6 7.5 %copy-start.6 = (s32[1,64,2]{1,2,0:T(2,128)S(1)}, s32[1,64,2]{1,2,0:T(2,128)}, u32[]{:S(2)}) copy-start(s32[1,64,2]{1,2,0:T(2,128)} %param.13) | copy-start | bytes 1540
  145.6 37.0 %all-to-all-start.2 = ((bf16[64,16,1152]{2,1,0:T(8,128)(2,1)}), bf16[64,16,1152]{2,1,0:T(8,128)(2,1)}, u32[]{:S(2)}, u32[]{:S(2)}) async-start(bf16[64,16,1152]{2,1,0:T(8,128)(2,1)} %bitcast.45), calls=%async_computation.2 | async-start | bytes 4718592 | tf_op jit(solution)/shard_map/all_to_all | solution.py:604
  152.1 1.1 copy-start.2
  182.6 22.5 %collective-permute-start = (bf16[1,64,3584]{2,1,0:T(8,128)(2,1)}, bf16[1,64,3584]{2,1,0:T(8,128)(2,1)S(1)}, u32[]{:S(2)}, u32[]{:S(2)}) collective-permute-start(bf16[1,64,3584]{2,1,0:T(8,128)(2,1)} %bitcast.53), channel_id=1, source_target_pairs={{0,64},{64,128},{128,192},{192,0},{1,65},{65,129},{129,193},{193,1... | collective-permute-start | bytes 1376264 | tf_op jit(solution)/shard_map/ppermute | solution.py:609
  191.3 24.2 %collective-permute-start.1 = (bf16[1,64,3584]{2,1,0:T(8,128)(2,1)}, bf16[1,64,3584]{2,1,0:T(8,128)(2,1)S(1)}, u32[]{:S(2)}, u32[]{:S(2)}) collective-permute-start(bf16[1,64,3584]{2,1,0:T(8,128)(2,1)} %bitcast.52), channel_id=1, source_target_pairs={{0,192},{64,0},{128,64},{192,128},{1,193},{65,1},{129,65},{193,129... | collective-permute-start | bytes 1376264 | tf_op jit(solution)/shard_map/ppermute | solution.py:609
